TPU v7x, 256 devices: a whole 4x4x8 slice. The times are simulated.
256 devices in a mesh: ctx: 64 (over y, x_hi, z), head: 4 (over x_lo, core).
Axes of the slice: x: 4 (x_hi: 2, x_lo: 2; x = x_hi * 2 + x_lo), y: 4, z: 8, core: 2. Of those that a mesh axis runs over, the one named last changes fastest.
Arguments:
- query_all: bfloat16 [8192, 1024], P('ctx', 'head'), may hold values from -6 to 6
- key_all: bfloat16 [8192, 1024], P('ctx', 'head'), may hold values from -6 to 6
- value_all: bfloat16 [8192, 1024], P('ctx', 'head'), may hold values from -6 to 6
- cotangent: bfloat16 [8192, 1024], P('ctx', 'head'), may hold values from -16 to 16
- conv_input: bfloat16 [8192, 1024], P('ctx', 'head'), may hold values from -6 to 6
- rec_lengths: int32 [3], replicated, may hold values from 1365 to 2730
- out_proj: bfloat16 [1024, 1024], P(None, 'head'), may hold values from -0.1875 to 0.1875
- conv_weight: bfloat16 [31, 1024], P(None, 'head'), may hold values from -1 to 1
Outputs:
- q_grad: bfloat16 [8192, 1024], P('ctx', 'head')
- k_grad: bfloat16 [8192, 1024], P('ctx', 'head')
- v_grad: bfloat16 [8192, 1024], P('ctx', 'head')
- x_grad: bfloat16 [8192, 1024], P('ctx', 'head')
- out_proj_grad: float32 [1024, 1024], P('ctx', 'head')
- conv_weight_grad: float32 [31, 1024], P(None, 'head')
Inputs may be any that keep to these rules, and one draw needn't show every extreme that they name: `rec_lengths`: the recordings lie end to end from frame 0; frames from their total on are padding.
All inputs are finite; a program needn't handle non-finite values.
Results may differ from a plain program's by a relative error of at most 0.03.
Values may be sent and summed in bfloat16 or wider, within the bound.
A program may use at most 64 MiB of HBM per device.

v0:
```python
import jax
import jax.numpy as jnp
from jax import lax
from jax.sharding import PartitionSpec as P

HEAD_DIM = 64


def extended_2(block, sides, width):
    for axis, dim in sides:
        count = lax.axis_size(axis)
        forward = [(i, i + 1) for i in range(count - 1)]
        backward = [(target, source) for source, target in forward]
        low = lax.ppermute(
            lax.slice_in_dim(block, block.shape[dim] - width, None, axis=dim), axis, forward
        )
        high = lax.ppermute(lax.slice_in_dim(block, 0, width, axis=dim), axis, backward)
        block = jnp.concatenate([low, block, high], axis=dim)
    return block


def split_heads(matrix):
    return matrix.reshape(matrix.shape[0], -1, HEAD_DIM)


def join_heads(tensor):
    return jnp.transpose(tensor, (1, 0, 2)).reshape(tensor.shape[1], -1)


def over_blocks(step_fn, running, members):
    row_count = members[0].shape[0]
    blocks = row_count // 512
    stacked = tuple((member.reshape((blocks, 512) + member.shape[1:]) for member in members))

    def inner_step(state, inputs):
        block_members, block_index = inputs
        return (step_fn(state, block_members, block_index * 512), None)

    running, unused = lax.scan(inner_step, running, (stacked, jnp.arange(blocks, dtype=jnp.int32)))
    return running


def conv_forward(extended, taps, frames):
    wide = extended.astype(jnp.float32)
    weights = taps.astype(jnp.float32)
    result = jnp.zeros((frames, extended.shape[1]), jnp.float32)
    for offset in range(taps.shape[0]):
        result = result + weights[offset] * wide[offset : offset + frames]
    return result


def conv_backward(grad_ext, taps, frames):
    wide = grad_ext.astype(jnp.float32)
    weights = taps.astype(jnp.float32)
    reach = taps.shape[0] - 1
    result = jnp.zeros((frames, grad_ext.shape[1]), jnp.float32)
    for offset in range(taps.shape[0]):
        result = result + weights[offset] * wide[reach - offset : reach - offset + frames]
    return result


def tap_products(grad_conv, extended):
    frames = grad_conv.shape[0]
    wide = extended.astype(jnp.float32)
    grad_wide = grad_conv.astype(jnp.float32)
    rows_out = [
        jnp.sum(grad_wide * wide[offset : offset + frames], axis=0)
        for offset in range(extended.shape[0] - frames + 1)
    ]
    return jnp.stack(rows_out)


def gate_slope(conv_out, upstream):
    sigmoid_value = jax.nn.sigmoid(conv_out)
    return (
        upstream.astype(jnp.float32) * sigmoid_value * (1.0 + conv_out * (1.0 - sigmoid_value))
    ).astype(jnp.bfloat16)


def on_device(
    query_all, key_all, value_all, cotangent, conv_input, rec_lengths, out_proj, conv_weight
):
    frames, local_width = query_all.shape
    half_taps = conv_weight.shape[0] // 2
    score_scale = HEAD_DIM ** (-0.5)
    valid_total = jnp.sum(rec_lengths)
    positions = lax.axis_index("ctx") * frames + jnp.arange(frames, dtype=jnp.int32)
    frame_ok = positions < valid_total
    masked = jnp.where(frame_ok[:, None], conv_input, jnp.zeros_like(conv_input))
    input_ext = extended_2(masked, (("ctx", 0),), half_taps)
    conv_out = conv_forward(input_ext, conv_weight, frames)
    grad_conv = gate_slope(conv_out, cotangent)
    grad_ext = extended_2(grad_conv, (("ctx", 0),), half_taps)
    conv_weight_grad = lax.psum(tap_products(grad_conv, input_ext), "ctx")
    grad_input = conv_backward(grad_ext, conv_weight, frames)
    x_grad = (cotangent.astype(jnp.float32) + jnp.where(frame_ok[:, None], grad_input, 0.0)).astype(
        jnp.bfloat16
    )
    full_grad = lax.all_gather(x_grad, "head", axis=1, tiled=True)
    grad_out16 = jnp.dot(full_grad, out_proj, preferred_element_type=jnp.float32).astype(
        jnp.bfloat16
    )
    query_heads = split_heads(query_all)
    grad_heads = split_heads(grad_out16)
    grad_wide = grad_heads.astype(jnp.float32)
    heads_here = query_heads.shape[1]
    start_max = jnp.full((heads_here, frames), -1e30, jnp.float32)
    zeros_sum = jnp.zeros((heads_here, frames), jnp.float32)
    zeros_acc = jnp.zeros((heads_here, frames, HEAD_DIM), jnp.float32)
    zeros_keys = jnp.zeros((frames, heads_here, HEAD_DIM), jnp.float32)

    def masked_scores(key_rows, first_row):
        scores = (
            jnp.einsum(
                "qhd,khd->hqk",
                query_heads,
                split_heads(key_rows),
                preferred_element_type=jnp.float32,
            )
            * score_scale
        )
        key_ok = first_row + jnp.arange(key_rows.shape[0], dtype=jnp.int32) < valid_total
        return jnp.where(key_ok[None, None, :], scores, -jnp.inf)

    def forward_step(running, members, first_row):
        maxima, totals, numer = running
        key_rows, value_rows = members
        scores = masked_scores(key_rows, first_row)
        new_max = jnp.maximum(maxima, jnp.max(scores, axis=-1))
        shrink = jnp.exp(maxima - new_max)
        weights = jnp.exp(scores - new_max[..., None])
        totals = totals * shrink + jnp.sum(weights, axis=-1)
        numer = numer * shrink[..., None] + jnp.einsum(
            "hqk,khd->hqd",
            weights.astype(jnp.bfloat16),
            split_heads(value_rows),
            preferred_element_type=jnp.float32,
        )
        return (new_max, totals, numer)

    maxima, totals, numer = over_blocks(
        forward_step,
        (start_max, zeros_sum, zeros_acc),
        (
            lax.all_gather(key_all, "ctx", axis=0, tiled=True),
            lax.all_gather(value_all, "ctx", axis=0, tiled=True),
        ),
    )
    attn_out = numer / totals[..., None]
    log_total = maxima + jnp.log(totals)
    row_delta = jnp.einsum("qhd,hqd->hq", grad_wide, attn_out)
    query_sum = None

    def query_step(running, members, first_row):
        key_rows, value_rows = members
        scores = masked_scores(key_rows, first_row)
        probs = jnp.exp(scores - log_total[..., None])
        slopes = jnp.einsum(
            "qhd,khd->hqk", grad_heads, split_heads(value_rows), preferred_element_type=jnp.float32
        )
        dscores = probs * (slopes - row_delta[..., None])
        return running + jnp.einsum(
            "hqk,khd->hqd",
            dscores,
            split_heads(key_rows).astype(jnp.float32),
            precision=lax.Precision.HIGHEST,
        )

    query_sum = over_blocks(
        query_step,
        zeros_acc,
        (
            lax.all_gather(key_all, "ctx", axis=0, tiled=True),
            lax.all_gather(value_all, "ctx", axis=0, tiled=True),
        ),
    )
    lse_all, delta_all = (
        lax.all_gather(log_total, "ctx", axis=1, tiled=True),
        lax.all_gather(row_delta, "ctx", axis=1, tiled=True),
    )
    key_heads = split_heads(key_all)
    value_heads = split_heads(value_all)

    def key_step(running, members, first_row):
        key_acc, value_acc = running
        query_rows, grad_rows = members
        rows_here = query_rows.shape[0]
        lse_rows = lax.dynamic_slice_in_dim(lse_all, first_row, rows_here, 1)
        delta_rows = lax.dynamic_slice_in_dim(delta_all, first_row, rows_here, 1)
        scores = (
            jnp.einsum(
                "qhd,khd->hqk",
                split_heads(query_rows),
                key_heads,
                preferred_element_type=jnp.float32,
            )
            * score_scale
        )
        scores = jnp.where(frame_ok[None, None, :], scores, -jnp.inf)
        probs = jnp.exp(scores - lse_rows[..., None])
        probs16 = probs.astype(jnp.bfloat16)
        slopes = jnp.einsum(
            "qhd,khd->hqk", split_heads(grad_rows), value_heads, preferred_element_type=jnp.float32
        )
        dscores16 = (probs * (slopes - delta_rows[..., None])).astype(jnp.bfloat16)
        key_acc = key_acc + jnp.einsum(
            "hqk,qhd->khd", dscores16, split_heads(query_rows), preferred_element_type=jnp.float32
        )
        value_acc = value_acc + jnp.einsum(
            "hqk,qhd->khd", probs16, split_heads(grad_rows), preferred_element_type=jnp.float32
        )
        return (key_acc, value_acc)

    key_sum, value_sum = over_blocks(
        key_step,
        (zeros_keys, zeros_keys),
        (
            lax.all_gather(query_all, "ctx", axis=0, tiled=True),
            lax.all_gather(grad_out16, "ctx", axis=0, tiled=True),
        ),
    )
    q_grad = join_heads(query_sum * score_scale).astype(jnp.bfloat16)
    attn16 = join_heads(attn_out).astype(jnp.bfloat16)
    k_grad = (key_sum * score_scale).reshape(frames, local_width).astype(jnp.bfloat16)
    v_grad = value_sum.reshape(frames, local_width).astype(jnp.bfloat16)
    out_proj_grad = lax.psum_scatter(
        jnp.einsum("ta,tb->ab", full_grad, attn16, preferred_element_type=jnp.float32),
        "ctx",
        scatter_dimension=0,
        tiled=True,
    )
    return (q_grad, k_grad, v_grad, x_grad, out_proj_grad, conv_weight_grad)


def solution(mesh):
    placed = (
        P("ctx", "head"),
        P("ctx", "head"),
        P("ctx", "head"),
        P("ctx", "head"),
        P("ctx", "head"),
        P(),
        P(None, "head"),
        P(None, "head"),
    )
    return jax.shard_map(
        on_device,
        mesh=mesh,
        in_specs=placed,
        out_specs=(
            P("ctx", "head"),
            P("ctx", "head"),
            P("ctx", "head"),
            P("ctx", "head"),
            P("ctx", "head"),
            P(None, "head"),
        ),
        check_vma=False,
    )
```

profile of v0, /device:TPU:2, one launch (start us, length us, event | category | flops | bytes accessed | tf_op | source)
XLA Modules:
  0.0 1256.9 jit_solution(8981451089153710377)
XLA Ops:
  9.5 1.3 reduce_sum.297
  12.4 1.3 collective-permute-start.1
  13.7 4.5 collective-permute-start
  23.2 1.8 fusion.57
  25.0 1.3 collective-permute-start.3
  26.3 4.5 collective-permute-start.2
  31.2 360.6 %psum.7 = f32[31,256]{1,0:T(8,128)} all-reduce(f32[31,256]{1,0:T(8,128)S(1)} %stack.127), channel_id=1, replica_groups=mesh['ctx'=64,'head'=4] {'ctx'}, use_global_device_ids=true, to_apply=%region_41.42 | all-reduce | flops 7936 | bytes 63488 | tf_op jit(solution)/shard_map/psum | solution.py:94
  392.3 5.8 all_gather.25
  399.1 6.4 copy.42
  405.5 6.4 copy.40
  411.9 61.1 %while.39 = (s32[]{:T(128)}, f32[4,128]{1,0:T(4,128)S(1)}, f32[4,128]{1,0:T(4,128)S(1)}, f32[4,128,64]{1,2,0:T(8,128)S(1)}, s32[16]{0:T(128)S(1)}, /*index=5*/s3...) while((s32[]{:T(128)}, f32[4,128]{1,0:T(4,128)S(1)}, ...), condition=%wide.region_4.5_spmd.clone, body=%wide.region_1.4_spmd.clone.sunk | while | flops 69045760 | bytes 5080237 | solution.py:39
  415.7 1.1 constant_dynamic-slice_fusion.12
  419.5 1.1 constant_dynamic-slice_fusion.12
  423.4 1.1 constant_dynamic-slice_fusion.12
  427.2 1.1 constant_dynamic-slice_fusion.12
  431.0 1.1 constant_dynamic-slice_fusion.12
  434.8 1.1 constant_dynamic-slice_fusion.12
  438.6 1.1 constant_dynamic-slice_fusion.12
  442.5 1.1 constant_dynamic-slice_fusion.12
  446.3 1.1 constant_dynamic-slice_fusion.12
  450.1 1.1 constant_dynamic-slice_fusion.12
  453.9 1.1 constant_dynamic-slice_fusion.12
  457.7 1.1 constant_dynamic-slice_fusion.12
  461.5 1.1 constant_dynamic-slice_fusion.12
  465.4 1.1 constant_dynamic-slice_fusion.12
  469.2 1.1 constant_dynamic-slice_fusion.12
  473.1 69.3 %while.40 = (s32[]{:T(128)}, f32[4,128,64]{1,2,0:T(8,128)S(1)}, s32[16]{0:T(128)S(1)}, s32[]{:T(128)}, bf16[16,512,256]{1,2,0:T(8,128)(2,1)}, /*index=5*/bf16[12...) while((s32[]{:T(128)}, f32[4,128,64]{1,2,0:T(8,128)S(1)}, ...), condition=%wide.region_6.7_spmd.clone, body=%wide.region_5.6_spmd.clone.sunk | while | flops 269812736 | bytes 6427827 | solution.py:39
  473.1 1.1 constant_dynamic-slice_fusion.13
  477.4 1.1 constant_dynamic-slice_fusion.13
  481.7 1.1 constant_dynamic-slice_fusion.13
  486.1 1.1 constant_dynamic-slice_fusion.13
  490.4 1.1 constant_dynamic-slice_fusion.13
  494.8 1.1 constant_dynamic-slice_fusion.13
  499.1 1.1 constant_dynamic-slice_fusion.13
  503.4 1.1 constant_dynamic-slice_fusion.13
  507.7 1.1 constant_dynamic-slice_fusion.13
  512.1 1.1 constant_dynamic-slice_fusion.13
  516.4 1.1 constant_dynamic-slice_fusion.13
  520.8 1.1 constant_dynamic-slice_fusion.13
  543.2 174.5 %all_gather.27 = f32[4,8192]{1,0:T(4,128)S(1)} all-gather(f32[4,128]{1,0:T(4,128)S(1)} %get-tuple-element.874), channel_id=1, replica_groups=mesh['ctx'=64,'head'=4] {'ctx'}, dimensions={1}, use_global_device_ids=true | all-gather | bytes 133120 | tf_op jit(solution)/shard_map/all_gather | solution.py:178
  717.7 176.5 %all_gather.29 = f32[4,8192]{1,0:T(4,128)S(1)} all-gather(f32[4,128]{1,0:T(4,128)S(1)} %get-tuple-element.873), channel_id=1, replica_groups=mesh['ctx'=64,'head'=4] {'ctx'}, dimensions={1}, use_global_device_ids=true | all-gather | bytes 133120 | tf_op jit(solution)/shard_map/all_gather | solution.py:179
  894.3 1.4 fusion.97
  895.7 75.7 %while.41 = (s32[]{:T(128)}, f32[128,4,64]{0,2,1:T(8,128)S(1)}, f32[128,4,64]{0,2,1:T(8,128)S(1)}, bf16[16,512,256]{2,1,0:T(8,128)(2,1)}, bf16[128,4,64]{0,2,1:T...) while((s32[]{:T(128)}, f32[128,4,64]{0,2,1:T(8,128)S(1)}, ...), condition=%wide.region_8.9_spmd.clone, body=%wide.region_7.8_spmd.clone.sunk | while | flops 136184064 | bytes 6996466 | solution.py:39
  919.4 1.1 constant_dynamic-slice_fusion.14
  933.6 1.1 constant_dynamic-slice_fusion.14
  952.5 1.1 constant_dynamic-slice_fusion.14
  966.7 1.1 constant_dynamic-slice_fusion.14
  973.0 277.4 %reduce-scatter.2.cloned.1.call-done = f32[16,256]{1,0:T(8,128)} async-done(((f32[1024,256]{1,0:T(8,128)}), f32[16,256]{1,0:T(8,128)}) %reduce-scatter.2.cloned.1.call-update) | async-done | bytes 16400 | tf_op jit(solution)/shard_map/reduce_scatter | solution.py:226
  (412 shorter events, 153.1 us)
Async XLA Ops:
  7.2 391.0 %copy-start = (bf16[1024,256]{1,0:T(8,128)(2,1)S(1)}, bf16[1024,256]{1,0:T(8,128)(2,1)}, u32[]{:S(2)}) copy-start(bf16[1024,256]{1,0:T(8,128)(2,1)} %param.20) | copy-start | bytes 1572868
  7.2 384.7 %copy-start.2 = (bf16[128,256]{1,0:T(8,128)(2,1)S(1)}, bf16[128,256]{1,0:T(8,128)(2,1)}, u32[]{:S(2)}) copy-start(bf16[128,256]{1,0:T(8,128)(2,1)} %param.17) | copy-start | bytes 196612
  7.2 391.9 %all-gather.5.cloned.1.call-start = ((), (), s32[]{:S(2)}) async-start(), calls=%async_computation.1 | async-start | bytes 4259840 | tf_op jit(solution)/shard_map/all_gather | solution.py:173
  7.9 397.6 %all-gather.7.cloned.1.call-start = ((), (), s32[]{:S(2)}) async-start(), calls=%async_computation.2 | async-start | bytes 4259840 | tf_op jit(solution)/shard_map/all_gather | solution.py:174
  8.7 887.0 %all-gather.9.cloned.1.call-start = ((), (), s32[]{:S(2)}) async-start(), calls=%async_computation.3 | async-start | bytes 4259840 | tf_op jit(solution)/shard_map/all_gather | solution.py:218
  9.4 886.3 %all-gather.11.cloned.1.call-start = ((), (), s32[]{:S(2)}) async-start(), calls=%async_computation.4 | async-start | bytes 4259840 | tf_op jit(solution)/shard_map/all_gather | solution.py:219
  12.4 10.8 collective-permute-start.1
  13.7 9.5 collective-permute-start
  25.0 366.8 %collective-permute-start.3 = (bf16[15,256]{1,0:T(8,128)(2,1)S(1)}, bf16[15,256]{1,0:T(8,128)(2,1)S(1)}, u32[]{:S(2)}, u32[]{:S(2)}) collective-permute-start(bf16[15,256]{1,0:T(8,128)(2,1)S(1)} %get-tuple-element.481), channel_id=1, source_target_pairs={{4,0},{8,4},{12,8},{16,12},{20,16},{24,20},{28,24},{32,28},{36,32}... | collective-permute-start | bytes 23048 | tf_op jit(solution)/shard_map/ppermute | solution.py:17
  26.3 365.5 %collective-permute-start.2 = (bf16[15,256]{1,0:T(8,128)(2,1)S(1)}, bf16[15,256]{1,0:T(8,128)(2,1)S(1)}, u32[]{:S(2)}, u32[]{:S(2)}) collective-permute-start(bf16[15,256]{1,0:T(8,128)(2,1)S(1)} %get-tuple-element.480), channel_id=1, source_target_pairs={{0,4},{4,8},{8,12},{12,16},{16,20},{20,24},{24,28},{28,32},{32,36}... | collective-permute-start | bytes 23048 | tf_op jit(solution)/shard_map/ppermute | solution.py:14
  392.3 13.2 %copy-start.3 = (bf16[128,256]{1,0:T(8,128)(2,1)}, bf16[128,256]{1,0:T(8,128)(2,1)S(1)}, u32[]{:S(2)}) copy-start(bf16[128,256]{1,0:T(8,128)(2,1)S(1)} %fusion.26) | copy-start | bytes 196612
  398.4 0.6 copy-start.1
  399.0 851.4 %reduce-scatter.2.cloned.1.call-start = ((), (), s32[]{:S(2)}) async-start(), calls=%async_computation.5 | async-start | bytes 1064960 | tf_op jit(solution)/shard_map/reduce_scatter | solution.py:226
Sparse Core Ops, SparseCore 0:
  11.5 130.4 all-gather.4
  145.5 124.9 all-gather.6
  274.1 125.7 all-gather.8
  403.8 124.9 all-gather.10
  895.8 354.5 reduce-scatter.1
where the time goes:
time: 1260 us
  blocking collectives  717 us (57%)
  waiting for transfers between devices  280 us (22%)
  local copies, waits for them, and re-layouts  105 us (8%)
  matrix products  56.5 us (4%)
  other arithmetic  39.9 us (3%)
  loops' own time  32.7 us (3%)
  between operations  14.1 us (1%)
    psum x1, blocking collectives, on_device(): conv_weight_grad = lax.psum(tap_products(grad_conv, input_ext), 'ctx')  361 us
    reduce_scatter x1, waiting for transfers between devices, on_device(): lax.psum_scatter(jnp.einsum('ta,tb->ab', full_grad, attn16, preferred_ele...  277 us
    all_gather x1, blocking collectives, on_device(): lax.all_gather(row_delta, 'ctx', axis=1, tiled=True)  177 us
    all_gather x1, blocking collectives, on_device(): lax.all_gather(log_total, 'ctx', axis=1, tiled=True)  175 us
    dynamic_slice x128, local copies, waits for them, and re-layouts, over_blocks(): lax.scan(inner_step, running, (stacked, jnp.arange(blocks, dtype=jnp.int3...  84 us
    another operation x3, loops' own time, over_blocks(): lax.scan(inner_step, running, (stacked, jnp.arange(blocks, dtype=jnp.int3...  32.7 us
  transfers between devices with their start and end apart: 9, of which 1 were waited for; matrix products, arithmetic and copies ran while one was open for 16% of the time, Pallas kernels for 0%

commit v1 on v0

v1 whole, which is shorter than its diff:
```python
import functools

import jax
import jax.numpy as jnp
from jax import lax
from jax.experimental import pallas as pl
from jax.experimental.pallas import tpu as pltpu
from jax.sharding import PartitionSpec as P

F32, BF16 = jnp.float32, jnp.bfloat16
HEAD_DIM = 64
ROWS = 128
WIDTH = 256
PAIR = 128
BLOCK = 256
TAPS = 31
NEG = -1e30
LOG2E = 1.4426950408889634
MESH = pl.DeviceIdType.MESH


def nt(a, b):
    return lax.dot_general(a, b, (((1,), (1,)), ((), ())), preferred_element_type=F32)


def tn(a, b):
    return lax.dot_general(a, b, (((0,), (0,)), ((), ())), preferred_element_type=F32)


def nn(a, b):
    return jnp.dot(a, b, preferred_element_type=F32)


def iota(shape, dim):
    return lax.broadcasted_iota(jnp.int32, shape, dim)


def fused_kernel(
    Y, Z,
    rec, q, k, v, ct, ci, w, taps,
    q_o, k_o, v_o, x_o, g_o, c_o,
    kv, qg, dog, kt, va, ka, vta, qta, probs, mk, mrun, ot, dot_, dqt, mst, lin, dlt, gbuf, dsb,
    hci, hct, ext, gex, xf, do_s,
    st, os, orr, of, ox, gs, gr, gy, gx, gt, gz, gzr,
    acc, rss, rsr, fk, dqs, dqr, fq,
    cwp, cwr, c1, cx, cz, cfin,
    halo_s, halo_r, head_s, head_r, xs, xr, ys, yr, kvs, kvr, rs_s, rs_r, gzs, gzrs, czs, czr,
):
    Q = Y * BLOCK
    N = 2 * Y * Z
    ctx, head = lax.axis_index("ctx"), lax.axis_index("head")
    y = lax.div(ctx, 2 * Z)
    xh = lax.rem(lax.div(ctx, Z), 2)
    z = lax.rem(ctx, Z)
    other = 1 - xh

    def at(yy, xx, zz):
        return ((yy * 2 + xx) * Z + zz, head)

    def y_peer(d):
        return at(lax.rem(y + d, Y), xh, z)

    def z_peer(d):
        return at(y, xh, lax.rem(z + d, Z))

    def head_peer(d):
        return (ctx, lax.rem(head + d, Y))

    partner = at(y, other, z)
    following = (lax.rem(ctx + 1, N), head)
    preceding = (lax.rem(ctx + N - 1, N), head)

    def remote(src, dst, send, recv, device):
        return pltpu.make_async_remote_copy(
            src_ref=src, dst_ref=dst, send_sem=send, recv_sem=recv, device_id=device, device_id_type=MESH
        )

    own_cols = pl.ds(pl.multiple_of(xh * PAIR, PAIR), PAIR)
    other_cols = pl.ds(pl.multiple_of(other * PAIR, PAIR), PAIR)

    def halo(i):
        src, dst, dev = (
            (ci.at[pl.ds(ROWS - 32, 32)], hci.at[0], following),
            (ci.at[pl.ds(0, 32)], hci.at[1], preceding),
            (ct.at[pl.ds(ROWS - 16, 16)], hct.at[0], following),
            (ct.at[pl.ds(0, 16)], hct.at[1], preceding),
        )[i]
        return remote(src, dst, halo_s.at[i], halo_r.at[i], dev)

    XK, XV, XQ, XDO, XO, XG, XDK, XDV, XDQ, XCW = range(10)

    def x_copy(i):
        src, dst = (
            lambda: (k.at[:, other_cols], kv.at[0, 0, xh]),
            lambda: (v.at[:, other_cols], kv.at[0, 1, xh]),
            lambda: (q.at[:, other_cols], qg.at[0, xh]),
            lambda: (do_s.at[:, other_cols], dog.at[0, xh]),
            lambda: (of.at[other], ox),
            lambda: (gy.at[other], gx),
            lambda: (fk.at[0, other], k_o.at[:, own_cols]),
            lambda: (fk.at[1, other], v_o.at[:, own_cols]),
            lambda: (fq.at[other], q_o.at[:, own_cols]),
            lambda: (c1, cx),
        )[i]()
        return remote(src, dst, xs.at[i], xr.at[i], partner)

    YQ, YDO, YST, YO, YG, YDQ, YC1, YC2 = range(8)

    def y_copy(i, d):
        src, dst = (
            lambda: (qg.at[0], qg.at[d]),
            lambda: (dog.at[0], dog.at[d]),
            lambda: (st.at[0], st.at[d]),
            lambda: (os.at[Y - d], orr.at[d]),
            lambda: (gs.at[lax.rem(y + d, Y)], gr.at[d]),
            lambda: (dqs.at[Y - d], dqr.at[d]),
            lambda: (cwp.at[lax.rem(y + d, Y)], cwr.at[d]),
            lambda: (cfin.at[y], cfin.at[y]),
        )[i]()
        return remote(src, dst, ys.at[i, d], yr.at[i, d], y_peer(d))

    def y_start(i):
        for d in range(1, Y):
            y_copy(i, d).start()

    def y_recv(i):
        for d in range(1, Y):
            y_copy(i, d).wait_recv()

    def kv_copy(slot):
        if isinstance(slot, int):
            up = slot <= Z // 2
            src, dev = (slot - 1, z_peer(1)) if up else ((slot + 1) % Z, z_peer(Z - 1))
            return remote(kv.at[src], kv.at[slot], kvs.at[slot], kvr.at[slot], dev)
        raise ValueError

    def rs_copy(s, dev):
        return remote(rss.at[s], rsr.at[s], rs_s.at[s], rs_r.at[s], dev)

    def gz_copy(d):
        return remote(gz.at[lax.rem(z + d, Z)], gzr.at[d], gzs.at[d], gzrs.at[d], z_peer(d))

    def cz_copy(d):
        return remote(cz.at[z], cz.at[z], czs.at[d], czr.at[d], z_peer(d))

    peers = [partner, following, preceding]
    peers += [y_peer(d) for d in range(1, Y)] + [z_peer(d) for d in range(1, Z)]
    peers += [head_peer(d) for d in range(1, Y)]
    barrier = pltpu.get_barrier_semaphore()
    for peer in peers:
        pl.semaphore_signal(barrier, inc=1, device_id=peer, device_id_type=MESH)
    pl.semaphore_wait(barrier, len(peers))

    for i in range(4):
        halo(i).start()
    for i in (XK, XV, XQ):
        x_copy(i).start()
    kv[0, 0, pl.ds(xh, 1)] = k[:, own_cols][None]
    kv[0, 1, pl.ds(xh, 1)] = v[:, own_cols][None]
    qg[0, pl.ds(xh, 1)] = q[:, own_cols][None]
    valid = rec[0] + rec[1] + rec[2]

    for i in (0, 1):
        halo(i).wait_recv()
    pos = ctx * ROWS - 32 + iota((ROWS + 64, WIDTH), 0)
    ext[...] = jnp.where(
        (pos >= 0) & (pos < valid), jnp.concatenate([hci[0], ci[...], hci[1]], axis=0).astype(F32), 0.0
    )
    for i in (2, 3):
        halo(i).wait_recv()
    weights = taps[...].astype(F32)
    for c in range(2):
        cols = slice(c * 128, c * 128 + 128)
        conv = jnp.zeros((ROWS + 32, 128), F32)
        for b in range(8):
            moved = ext[b : b + ROWS + 56, cols]
            for a in range(4):
                j = 8 * a + b - 1
                if 0 <= j < TAPS:
                    conv = conv + weights[j : j + 1, cols] * moved[8 * a : 8 * a + ROWS + 32]
        sig = jax.nn.sigmoid(conv)
        up = jnp.concatenate([hct[0, :, cols], ct[:, cols], hct[1, :, cols]], axis=0).astype(F32)
        slope = (up * sig * (1.0 + conv * (1.0 - sig))).astype(BF16).astype(F32)
        gpos = ctx * ROWS - 16 + iota((ROWS + 32, 128), 0)
        gex[:, cols] = jnp.where((gpos >= 0) & (gpos < N * ROWS), slope, 0.0)

    for i in (XK, XV):
        x_copy(i).wait_recv()
    kv_copy(1).start()
    kv_copy(Z - 1).start()
    x_copy(XQ).wait_recv()
    y_start(YQ)

    for c in range(2):
        cols = slice(c * 128, c * 128 + 128)
        back = jnp.zeros((ROWS, 128), F32)
        for b in range(8):
            moved = gex[b : b + ROWS + 24, cols]
            for a in range(4):
                j = TAPS - 8 * a - b
                if 0 <= j < TAPS:
                    back = back + weights[j : j + 1, cols] * moved[8 * a : 8 * a + ROWS]
        frame = ctx * ROWS + iota((ROWS, 128), 0)
        x16 = (ct[:, cols].astype(F32) + jnp.where(frame < valid, back, 0.0)).astype(BF16)
        x_o[:, cols] = x16
        xf[pl.ds(head, 1), :, cols] = x16[None]

    def head_copy(d, slot):
        return remote(xf.at[slot], xf.at[slot], head_s.at[d], head_r.at[d], head_peer(d))

    for d in range(1, Y):
        head_copy(d, head).start()

    crow = 32 // Y
    for c in range(2):
        cols = slice(c * 128, c * 128 + 128)
        grad = gex[16 : 16 + ROWS, cols]
        for b in range(8):
            moved = ext[b : b + ROWS + 40, cols]
            for a in range(2, 6):
                j = 8 * a + b - 17
                if 0 <= j < TAPS:
                    cwp[j // crow, j % crow : j % crow + 1, cols] = jnp.sum(
                        grad * moved[8 * a : 8 * a + ROWS], axis=0, keepdims=True
                    )
        cwp[Y - 1, crow - 1 : crow, cols] = jnp.zeros((1, 128), F32)
    y_start(YC1)

    for d in range(1, Y):
        head_copy(d, lax.rem(head + Y - d, Y)).wait_recv()
    grad_out = jnp.zeros((ROWS, WIDTH), F32)
    for h in range(Y):
        grad_out = grad_out + nn(xf[h], w[h * WIDTH : (h + 1) * WIDTH, :])
    do_s[...] = grad_out.astype(BF16)
    x_copy(XDO).start()
    dog[0, pl.ds(xh, 1)] = do_s[:, own_cols][None]

    y_recv(YQ)
    first_row = jnp.where(iota((16, BLOCK), 0) == 0, 1.0, 0.0).astype(BF16)
    zero_rows = jnp.zeros((112, BLOCK), BF16)
    for c in range(Y):
        cols = slice(c * BLOCK, (c + 1) * BLOCK)
        scaled = jnp.transpose(qg[c].reshape(BLOCK, PAIR).astype(F32) * (LOG2E * HEAD_DIM**-0.5))
        high = scaled.astype(BF16)
        low = (scaled - high.astype(F32)).astype(BF16)
        for h in range(2):
            rows = slice(h * HEAD_DIM, (h + 1) * HEAD_DIM)
            qta[h, :, cols] = jnp.concatenate([high[rows], low[rows], first_row, zero_rows], axis=0)
    mrun[...] = jnp.full(mrun.shape, NEG, F32)
    ot[...] = jnp.zeros(ot.shape, F32)
    ones_rows = jnp.ones((16, BLOCK), BF16)
    lane = iota((BLOCK, PAIR), 1)

    x_copy(XDO).wait_recv()
    y_start(YDO)

    def forward_step(s, carry):
        i = lax.div(s, 2)
        odd = lax.rem(s, 2)
        slot = lax.rem(odd * (i + 1) + (1 - odd) * (Z - i), Z)

        @pl.when(s > 0)
        def _():
            remote(kv.at[slot], kv.at[slot], kvs.at[slot], kvr.at[slot], z_peer(1)).wait_recv()

        @pl.when((odd == 1) & (s < Z - 1))
        def _():
            remote(kv.at[slot], kv.at[slot + 1], kvs.at[slot + 1], kvr.at[slot + 1], z_peer(1)).start()

        @pl.when((odd == 0) & (s > 0) & (s < Z - 2))
        def _():
            remote(kv.at[slot], kv.at[slot - 1], kvs.at[slot - 1], kvr.at[slot - 1], z_peer(Z - 1)).start()

        keys = kv[slot, 0].reshape(BLOCK, PAIR).astype(F32)
        values = kv[slot, 1].reshape(BLOCK, PAIR).astype(F32)
        kt[slot] = jnp.transpose(keys).astype(BF16)
        values_t = jnp.transpose(values).astype(BF16)
        keys_moved = pltpu.roll(keys, HEAD_DIM, 1)
        values_moved = pltpu.roll(values, HEAD_DIM, 1)
        origin = lax.rem(z + Z - slot, Z)
        row = iota((BLOCK, PAIR), 0)
        position = (y * 2 * Z + origin) * ROWS + lax.div(row, ROWS) * (Z * ROWS) + lax.rem(row, ROWS)
        bias = jnp.where((lane == 0) & (position >= valid), NEG, 0.0).astype(BF16)
        for h in range(2):
            first, second = (keys, keys_moved) if h == 0 else (keys_moved, keys)
            ka[h] = jnp.concatenate([jnp.where(lane < HEAD_DIM, first, second).astype(BF16), bias], axis=1)
            mine = values if h == 0 else values_moved
            extra = jnp.where(lane < HEAD_DIM + 2, 1.0, 0.0)
            va[slot, h] = jnp.where(lane < HEAD_DIM, mine, extra).astype(BF16)
            vta[h] = jnp.concatenate([values_t[h * HEAD_DIM : (h + 1) * HEAD_DIM], ones_rows], axis=0)
        for h in range(2):
            for c in range(Y):
                cols = slice(c * BLOCK, (c + 1) * BLOCK)
                scores = nn(ka[h], qta[h, :, cols])
                old = mrun[h, :, cols]
                new = jnp.maximum(old, jnp.max(scores, axis=0, keepdims=True))
                p16 = jnp.exp2(scores - new).astype(BF16)
                probs[slot, h, :, cols] = p16
                ot[h, :, cols] = ot[h, :, cols] * jnp.exp2(old - new) + nn(vta[h], p16)
                mrun[h, :, cols] = new
                mk[slot, h, :, cols] = new
        return carry

    lax.fori_loop(0, Z, forward_step, 0)

    y_recv(YDO)
    for c in range(Y):
        cols = slice(c * BLOCK, (c + 1) * BLOCK)
        dot_[:, cols] = jnp.transpose(dog[c].reshape(BLOCK, PAIR).astype(F32))
        for h in range(2):
            st[0, c, 3 * h : 3 * h + 1, :] = mrun[h, :, cols]
            st[0, c, 3 * h + 1 : 3 * h + 2, :] = ot[h, HEAD_DIM : HEAD_DIM + 1, cols]
            st[0, c, 3 * h + 2 : 3 * h + 3, :] = jnp.sum(
                ot[h, 0:HEAD_DIM, cols] * dot_[h * HEAD_DIM : (h + 1) * HEAD_DIM, cols], axis=0, keepdims=True
            )
        st[0, c, 6:8, :] = jnp.zeros((2, BLOCK), F32)
    y_start(YST)

    y_recv(YC1)
    total = cwp[y]
    for d in range(1, Y):
        total = total + cwr[d]
    c1[...] = total
    x_copy(XCW).start()
    dqt[...] = jnp.zeros(dqt.shape, F32)

    y_recv(YST)
    for c in range(Y):
        cols = slice(c * BLOCK, (c + 1) * BLOCK)
        parts = []
        for h in range(2):
            rows = [st[e, (c - e) % Y] for e in range(Y)]
            maxima = [r[3 * h : 3 * h + 1] for r in rows]
            top = functools.reduce(jnp.maximum, maxima)
            shrink = [jnp.exp2(m - top) for m in maxima]
            total = sum(r[3 * h + 1 : 3 * h + 2] * f for r, f in zip(rows, shrink))
            delta = sum(r[3 * h + 2 : 3 * h + 3] * f for r, f in zip(rows, shrink))
            inverse = 1.0 / total
            mst[h, :, cols] = top
            lin[h, :, cols] = inverse
            dlt[h, :, cols] = delta * inverse
            parts.append(ot[h, 0:HEAD_DIM, cols] * (shrink[0] * inverse))
        os[c] = jnp.transpose(jnp.concatenate(parts, axis=0)).astype(BF16)
    y_start(YO)

    delta_row = iota((16, BLOCK), 0)
    gbuf[...] = jnp.zeros(gbuf.shape, BF16)

    def backward_step(s, carry):
        i = lax.div(s, 2)
        odd = lax.rem(s, 2)
        slot = odd * (Z // 2 - 1 - i) + (1 - odd) * (Z // 2 + i)
        dk, dv = [], []
        for h in range(2):
            rows = slice(h * HEAD_DIM, (h + 1) * HEAD_DIM)
            for c in range(Y):
                cols = slice(c * BLOCK, (c + 1) * BLOCK)
                factor = jnp.exp2(mk[slot, h, :, cols] - mst[h, :, cols]) * lin[h, :, cols]
                shift = -dlt[h, :, cols] * factor
                high = shift.astype(BF16).astype(F32)
                gbuf[h, 0:HEAD_DIM, cols] = (dot_[rows, cols] * factor).astype(BF16)
                gbuf[h, HEAD_DIM : HEAD_DIM + 16, cols] = jnp.where(
                    delta_row == 0, high, jnp.where(delta_row == 1, shift - high, 0.0)
                ).astype(BF16)
                slopes = nn(va[slot, h], gbuf[h, :, cols])
                ds = (probs[slot, h, :, cols].astype(F32) * slopes).astype(BF16)
                dsb[h, :, cols] = ds
                dqt[rows, cols] += nn(kt[slot, rows, :], ds)
            dv.append(nt(probs[slot, h], gbuf[h, 0:HEAD_DIM, :]))
            dk.append(nn(dsb[h], qg[...].reshape(Q, PAIR)))
        acc[0] = jnp.where(lane < HEAD_DIM, dk[0], dk[1]) * HEAD_DIM**-0.5
        acc[1] = jnp.concatenate(dv, axis=1)

        @pl.when(s >= 2)
        def _():
            rs_copy(s - 2, z_peer(1)).wait_recv()
            acc[...] += rsr[s - 2].astype(F32)

        @pl.when(s < Z - 1)
        def _():
            rss[s] = acc[...].astype(BF16)
            rs_copy(s, at(y, xh, lax.rem(z + 1 + odd * (Z - 2), Z))).start()

        @pl.when(s == 0)
        def _():
            x_copy(XCW).wait_recv()
            cz[pl.ds(z, 1)] = (c1[...] + cx[...])[None]
            for d in range(1, Z):
                cz_copy(d).start()
            y_recv(YO)
            out = os[0].astype(F32)
            for d in range(1, Y):
                out = out + orr[d].astype(F32)
            of[...] = out.astype(BF16).reshape(2, ROWS, PAIR)
            x_copy(XO).start()

        @pl.when(s == 1)
        def _():
            x_copy(XO).wait_recv()
            mine, theirs = of[pl.ds(xh, 1)].reshape(ROWS, PAIR), ox[...]
            low = jnp.where(xh == 0, mine.astype(F32), theirs.astype(F32))
            high = jnp.where(xh == 0, theirs.astype(F32), mine.astype(F32))
            attn = jnp.concatenate([low, high], axis=1).astype(BF16)
            for h in range(Y):
                gs[h] = tn(xf[h], attn).astype(BF16).reshape(2, ROWS, WIDTH)
            y_start(YG)

        @pl.when(s == Z - 4)
        def _():
            y_recv(YG)
            sums = gs[pl.ds(y, 1)].reshape(2, ROWS, WIDTH).astype(F32)
            for d in range(1, Y):
                sums = sums + gr[d].astype(F32)
            gy[...] = sums.astype(BF16)
            x_copy(XG).start()
            for d in range(1, Z):
                remote(
                    cz.at[z], cz.at[lax.rem(z + Z - d, Z)], czs.at[d], czr.at[d], z_peer(d)
                ).wait_recv()
            total = cz[0]
            for d in range(1, Z):
                total = total + cz[d]
            cfin[pl.ds(y, 1)] = total[None]
            y_start(YC2)

        @pl.when(s == Z - 3)
        def _():
            x_copy(XG).wait_recv()
            sums = gy[pl.ds(xh, 1)].reshape(ROWS, WIDTH).astype(F32) + gx[...].astype(F32)
            sums = sums.reshape(Z, ROWS // Z, WIDTH)
            gt[...] = sums
            gz[...] = sums.astype(BF16)
            for d in range(1, Z):
                gz_copy(d).start()

        @pl.when(s == Z - 1)
        def _():
            for d in range(1, Z):
                gz_copy(d).wait_recv()
            sums = gt[pl.ds(z, 1)].reshape(ROWS // Z, WIDTH)
            for d in range(1, Z):
                sums = sums + gzr[d].astype(F32)
            g_o[...] = sums

        return carry

    lax.fori_loop(0, Z, backward_step, 0)

    for c in list(range(1, Y)) + [0]:
        dqs[c] = jnp.transpose(dqt[:, c * BLOCK : (c + 1) * BLOCK] * HEAD_DIM**-0.5).astype(BF16)
        if c:
            y_copy(YDQ, Y - c).start()
    rs_copy(Z - 2, z_peer(1)).wait_recv()
    fk[...] = (acc[...] + rsr[Z - 2].astype(F32)).astype(BF16).reshape(2, 2, ROWS, PAIR)
    x_copy(XDK).start()
    x_copy(XDV).start()
    k_o[:, own_cols] = fk[0, pl.ds(xh, 1)].reshape(ROWS, PAIR)
    v_o[:, own_cols] = fk[1, pl.ds(xh, 1)].reshape(ROWS, PAIR)

    for d in range(1, Y):
        slot = lax.rem(y + Y - d, Y)
        remote(cfin.at[slot], cfin.at[slot], ys.at[YC2, d], yr.at[YC2, d], y_peer(d)).wait_recv()
    for h in range(Y):
        count = min(crow, TAPS - h * crow)
        c_o[h * crow : h * crow + count, :] = cfin[h, 0:count, :]

    y_recv(YDQ)
    total = dqs[0].astype(F32)
    for d in range(1, Y):
        total = total + dqr[d].astype(F32)
    fq[...] = total.astype(BF16).reshape(2, ROWS, PAIR)
    x_copy(XDQ).start()
    q_o[:, own_cols] = fq[pl.ds(xh, 1)].reshape(ROWS, PAIR)

    for i in (XDK, XDV, XDQ):
        x_copy(i).wait_recv()
    for i in range(4):
        halo(i).wait_send()
    for i in range(10):
        x_copy(i).wait_send()
    for i in range(8):
        for d in range(1, Y):
            y_copy(i, d).wait_send()
    for d in range(1, Y):
        head_copy(d, head).wait_send()
    for slot in range(1, Z):
        kv_copy(slot).wait_send()
    for s in range(Z - 1):
        rs_copy(s, z_peer(1)).wait_send()
    for d in range(1, Z):
        gz_copy(d).wait_send()
        cz_copy(d).wait_send()


def on_device(Y, Z, query_all, key_all, value_all, cotangent, conv_input, rec_lengths, out_proj, conv_weight):
    Q = Y * BLOCK
    vm, dma = pltpu.VMEM, pltpu.SemaphoreType.DMA
    vmem = pl.BlockSpec(memory_space=pltpu.VMEM)
    crow = 32 // Y
    block = (ROWS, WIDTH)
    scratch = [
        vm((Z, 2, 2, ROWS, PAIR), BF16),
        vm((Y, 2, ROWS, PAIR), BF16),
        vm((Y, 2, ROWS, PAIR), BF16),
        vm((Z, PAIR, BLOCK), BF16),
        vm((Z, 2, BLOCK, PAIR), BF16),
        vm((2, BLOCK, 2 * PAIR), BF16),
        vm((2, HEAD_DIM + 16, BLOCK), BF16),
        vm((2, 2 * PAIR, Q), BF16),
        vm((Z, 2, BLOCK, Q), BF16),
        vm((Z, 2, 1, Q), F32),
        vm((2, 1, Q), F32),
        vm((2, HEAD_DIM + 16, Q), F32),
        vm((PAIR, Q), F32),
        vm((PAIR, Q), F32),
        vm((2, 1, Q), F32),
        vm((2, 1, Q), F32),
        vm((2, 1, Q), F32),
        vm((2, PAIR, Q), BF16),
        vm((2, BLOCK, Q), BF16),
        vm((2, 32, WIDTH), BF16),
        vm((2, 16, WIDTH), BF16),
        vm((ROWS + 64, WIDTH), F32),
        vm((ROWS + 32, WIDTH), F32),
        vm((Y, ROWS, WIDTH), BF16),
        vm(block, BF16),
        vm((Y, Y, 8, BLOCK), F32),
        vm((Y, BLOCK, PAIR), BF16),
        vm((Y, BLOCK, PAIR), BF16),
        vm((2, ROWS, PAIR), BF16),
        vm((ROWS, PAIR), BF16),
        vm((Y, 2, ROWS, WIDTH), BF16),
        vm((Y, 2, ROWS, WIDTH), BF16),
        vm((2, ROWS, WIDTH), BF16),
        vm(block, BF16),
        vm((Z, ROWS // Z, WIDTH), F32),
        vm((Z, ROWS // Z, WIDTH), BF16),
        vm((Z, ROWS // Z, WIDTH), BF16),
        vm((2, BLOCK, PAIR), F32),
        vm((Z, 2, BLOCK, PAIR), BF16),
        vm((Z, 2, BLOCK, PAIR), BF16),
        vm((2, 2, ROWS, PAIR), BF16),
        vm((Y, BLOCK, PAIR), BF16),
        vm((Y, BLOCK, PAIR), BF16),
        vm((2, ROWS, PAIR), BF16),
        vm((Y, crow, WIDTH), F32),
        vm((Y, crow, WIDTH), F32),
        vm((crow, WIDTH), F32),
        vm((crow, WIDTH), F32),
        vm((Z, crow, WIDTH), F32),
        vm((Y, crow, WIDTH), F32),
        dma((4,)), dma((4,)),
        dma((Y,)), dma((Y,)),
        dma((10,)), dma((10,)),
        dma((8, Y)), dma((8, Y)),
        dma((Z,)), dma((Z,)),
        dma((Z,)), dma((Z,)),
        dma((Z,)), dma((Z,)),
        dma((Z,)), dma((Z,)),
    ]
    return pl.pallas_call(
        functools.partial(fused_kernel, Y, Z),
        out_shape=(
            jax.ShapeDtypeStruct(block, BF16),
            jax.ShapeDtypeStruct(block, BF16),
            jax.ShapeDtypeStruct(block, BF16),
            jax.ShapeDtypeStruct(block, BF16),
            jax.ShapeDtypeStruct((ROWS // Z, WIDTH), F32),
            jax.ShapeDtypeStruct((TAPS, WIDTH), F32),
        ),
        in_specs=[pl.BlockSpec(memory_space=pltpu.SMEM)] + [vmem] * 7,
        out_specs=(vmem,) * 6,
        scratch_shapes=scratch,
        compiler_params=pltpu.CompilerParams(
            collective_id=0, has_side_effects=True, vmem_limit_bytes=56 * 1024 * 1024
        ),
        name="conv_attention_backward",
    )(rec_lengths, query_all, key_all, value_all, cotangent, conv_input, out_proj, conv_weight)


def solution(mesh):
    sizes = dict(mesh.shape)
    Y = sizes["head"]
    Z = sizes["ctx"] // (2 * Y)
    both = P("ctx", "head")
    return jax.shard_map(
        functools.partial(on_device, Y, Z),
        mesh=mesh,
        in_specs=(both, both, both, both, both, P(), P(None, "head"), P(None, "head")),
        out_specs=(both, both, both, both, both, P(None, "head")),
        check_vma=False,
    )
```

time: 1260 us -> 92.1 us (0.07)
  blocking collectives: 717 us -> 0 us
  waiting for transfers between devices: 280 us -> 0 us
  local copies, waits for them, and re-layouts: 105 us -> 5.33 us
  Pallas kernels: 0 us -> 84.3 us
  matrix products: 56.5 us -> 0 us
  other arithmetic: 39.9 us -> 0 us
  loops' own time: 32.7 us -> 0 us
  between operations: 14.1 us -> 0.66 us
    psum x1 -> x0, blocking collectives: 361 us -> none  [on_device(): conv_weight_grad = lax.psum(tap_products(grad_conv, input_ext), 'ctx')]
    all_gather x3 -> x0, blocking collectives: 357 us -> none  [the longest x1 177 us: on_device(): lax.all_gather(row_delta, 'ctx', axis=1, tiled=True)]
    reduce_scatter x1 -> x0, waiting for transfers between devices: 277 us -> none  [on_device(): lax.psum_scatter(jnp.einsum('ta,tb->ab', full_grad, attn16, preferred_ele...]
    pallas_call x0 -> x1, Pallas kernels: none -> 84.3 us  [on_device(): pl.pallas_call(functools.partial(fused_kernel, Y, Z), out_shape=(jax.Shap...]
    dynamic_slice x144 -> x0, local copies, waits for them, and re-layouts: 84.2 us -> none  [the longest x128 84 us: over_blocks(): lax.scan(inner_step, running, (stacked, jnp.arange(blocks, dtype=jnp.int3...]
    dot_general x130 -> x0, matrix products: 56.5 us -> none  [the longest x32 13.2 us: masked_scores(): jnp.einsum('qhd,khd->hqk', query_heads, split_heads(key_rows), preferred_...]
    another operation x3 -> x0, loops' own time: 32.7 us -> none  [over_blocks(): lax.scan(inner_step, running, (stacked, jnp.arange(blocks, dtype=jnp.int3...]
    lt x49 -> x0, other arithmetic: 32 us -> none  [the longest x32 20.9 us: masked_scores(): first_row + jnp.arange(key_rows.shape[0], dtype=jnp.int32) < valid_total]
  transfers between devices with their start and end apart: 9 -> 0, of which waited for: 1 -> 0; matrix products, arithmetic and copies ran while one was open for 16% -> 0% of each run, Pallas kernels for 0% -> 0%
where the time goes in v1:
time: 92.1 us; the launch traced here: 90.3 us
  Pallas kernels  84.3 us (92%)
  local copies, waits for them, and re-layouts  5.33 us (6%)
    pallas_call x1, Pallas kernels, on_device(): pl.pallas_call(functools.partial(fused_kernel, Y, Z), out_shape=(jax.Shap...  84.3 us
    unnamed x16, local copies, waits for them, and re-layouts  5.33 us

profile of v1, /device:TPU:2, one launch (start us, length us, event | category | flops | bytes accessed | tf_op | source)
XLA Modules:
  0.0 90.3 jit_solution(7721917886190788861)
XLA Ops:
  0.6 84.3 %conv_attention_backward.1 = (bf16[128,256]{1,0:T(8,128)(2,1)}, bf16[128,256]{1,0:T(8,128)(2,1)}, bf16[128,256]{1,0:T(8,128)(2,1)}, bf16[128,256]{1,0:T(8,128)(2...) custom-call(s32[3]{0:T(128)} %rec.1, bf16[128,256]{1,0:T(8,128)(2,1)} %q.1, bf16[128,256]{1,0:T(8,128)(2,1)} %k.1, ...), custom_call_target="tpu_custom_call" | custom-call | tf_op jit(solution)/shard_map/conv_attention_backward/pallas_call | solution.py:561
  84.9 0.0 copy-start.2
  84.9 1.5 %copy.20 = bf16[128,256]{1,0:T(8,128)(2,1)} copy(bf16[128,256]{1,0:T(8,128)(2,1)} %get-tuple-element.12) | data formatting | bytes 131072
  86.4 0.0 copy-done.2
  86.4 0.0 copy-start.1
  86.4 0.6 copy.21
  87.1 0.2 copy-done.1
  87.3 0.0 copy-start
  87.3 0.6 copy.22
  87.9 0.2 copy-done
  88.2 0.0 copy-start.4
  88.2 0.6 copy.23
  88.8 0.1 copy-done.4
  88.9 0.0 copy-start.3
  88.9 0.6 copy.24
  89.5 0.2 copy-done.3
  89.6 0.6 copy.25
Async XLA Ops:
  84.9 1.5 %copy-start.2 = (bf16[128,256]{1,0:T(8,128)(2,1)S(1)}, bf16[128,256]{1,0:T(8,128)(2,1)}, u32[]{:S(2)}) copy-start(bf16[128,256]{1,0:T(8,128)(2,1)} %get-tuple-element.13) | copy-start | bytes 196612
  86.4 0.9 copy-start.1
  87.3 0.9 copy-start
  88.2 0.7 copy-start.4
  88.9 0.8 copy-start.3

commit v2 on v1

v2 whole, which is shorter than its diff:
```python
import functools

import jax
import jax.numpy as jnp
from jax import lax
from jax.experimental import pallas as pl
from jax.experimental.pallas import tpu as pltpu
from jax.sharding import PartitionSpec as P

F32, BF16 = jnp.float32, jnp.bfloat16
HEAD_DIM = 64
ROWS = 128
WIDTH = 256
PAIR = 128
BLOCK = 256
TAPS = 31
NEG = -1e30
LOG2E = 1.4426950408889634
MESH = pl.DeviceIdType.MESH


def nt(a, b):
    return lax.dot_general(a, b, (((1,), (1,)), ((), ())), preferred_element_type=F32)


def tn(a, b):
    return lax.dot_general(a, b, (((0,), (0,)), ((), ())), preferred_element_type=F32)


def nn(a, b):
    return jnp.dot(a, b, preferred_element_type=F32)


def iota(shape, dim):
    return lax.broadcasted_iota(jnp.int32, shape, dim)


def fused_kernel(
    Y, Z,
    rec, q_in, k_in, v_in, ct_in, ci_in, w_in, taps,
    q_out, k_out, v_out, x_out, g_out, c_out,
    q, k, v, ct, ci, w, q_o, k_o, v_o, x_o, g_o, c_o, load_s, store_s,
    kv, qg, dog, kt, va, ka, vta, qta, probs, mk, mrun, ot, dot_, dqt, mst, lin, dlt, wts, gbuf, dsb,
    hci, hct, ext, gex, xf, xfp, do_s,
    st, os, orr, attn, gs, gr, gt, gz, gzr,
    part, rss, rsr, fin, dqs, dqr,
    cwp, cwr, c1, cx, cz, cfin,
    halo_s, halo_r, head_s, head_r, xs, xr, ys, yr, yxs, yxr, kvs, kvr, rs_s, rs_r, fin_s, fin_r, gzs, gzrs, czs, czr,
):
    Q = Y * BLOCK
    N = 2 * Y * Z
    HALF = Z // 2
    ctx, head = lax.axis_index("ctx"), lax.axis_index("head")
    y = lax.div(ctx, 2 * Z)
    xh = lax.rem(lax.div(ctx, Z), 2)
    z = lax.rem(ctx, Z)
    other = 1 - xh
    sides = (xh, other)

    def at(yy, xx, zz):
        return ((yy * 2 + xx) * Z + zz, head)

    def plus_y(d):
        return lax.rem(y + d, Y)

    def plus_z(d):
        return lax.rem(z + d, Z)

    def y_peer(d):
        return at(plus_y(d), xh, z)

    def z_peer(d):
        return at(y, xh, plus_z(d))

    def head_peer(d):
        return (ctx, lax.rem(head + d, Y))

    partner = at(y, other, z)
    following = (lax.rem(ctx + 1, N), head)
    preceding = (lax.rem(ctx + N - 1, N), head)

    def remote(src, dst, send, recv, device):
        return pltpu.make_async_remote_copy(
            src_ref=src, dst_ref=dst, send_sem=send, recv_sem=recv, device_id=device, device_id_type=MESH
        )

    own_cols = pl.ds(pl.multiple_of(xh * PAIR, PAIR), PAIR)
    other_cols = pl.ds(pl.multiple_of(other * PAIR, PAIR), PAIR)
    side_cols = (own_cols, other_cols)

    def halo(i):
        src, dst, dev = (
            (ci.at[pl.ds(ROWS - 32, 32)], hci.at[0], following),
            (ci.at[pl.ds(0, 32)], hci.at[1], preceding),
            (ct.at[pl.ds(ROWS - 16, 16)], hct.at[0], following),
            (ct.at[pl.ds(0, 16)], hct.at[1], preceding),
        )[i]
        return remote(src, dst, halo_s.at[i], halo_r.at[i], dev)

    XK, XV, XQ, XF, XCW = range(5)

    def x_copy(i):
        src, dst = (
            lambda: (k.at[:, other_cols], kv.at[0, 0, xh]),
            lambda: (v.at[:, other_cols], kv.at[0, 1, xh]),
            lambda: (q.at[:, other_cols], qg.at[0, xh]),
            lambda: (xf, xfp),
            lambda: (c1, cx),
        )[i]()
        return remote(src, dst, xs.at[i], xr.at[i], partner)

    def x_recv(i):
        if i < XF:
            dst = (kv.at[0, 0, other], kv.at[0, 1, other], qg.at[0, other])[i]
            remote(dst, dst, xs.at[i], xr.at[i], partner).wait_recv()
        else:
            x_copy(i).wait_recv()

    YQ, YST, YO, YG, YC1, YC2 = range(6)

    def y_copy(i, d):
        src, dst = (
            lambda: (qg.at[0], qg.at[d]),
            lambda: (st.at[0], st.at[d]),
            lambda: (os.at[Y - d], orr.at[d]),
            lambda: (gs.at[plus_y(d)], gr.at[d]),
            lambda: (cwp.at[plus_y(d)], cwr.at[d]),
            lambda: (cfin.at[y], cfin.at[y]),
        )[i]()
        return remote(src, dst, ys.at[i, d], yr.at[i, d], y_peer(d))

    def y_start(i):
        for d in range(1, Y):
            y_copy(i, d).start()

    def y_recv(i):
        for d in range(1, Y):
            y_copy(i, d).wait_recv()

    spread = [(d, e) for d in range(Y) for e in range(2) if d or e]
    SDO, SDQ = range(2)

    def spread_copy(i, d, e):
        src, dst = (
            lambda: (do_s.at[:, side_cols[e]], dog.at[d, xh]),
            lambda: (dqs.at[(Y - d) % Y, sides[e]], dqr.at[d, e]),
        )[i]()
        return remote(src, dst, yxs.at[i, d, e], yxr.at[i, d, e], at(plus_y(d), sides[e], z))

    def spread_recv(i):
        for d, e in spread:
            dst = dog.at[d, sides[e]] if i == SDO else dqr.at[d, e]
            remote(dst, dst, yxs.at[i, d, e], yxr.at[i, d, e], partner).wait_recv()

    def ring(src, dst, j, device):
        piece = (j % 2, sides[j // 2])
        return remote(kv.at[(src, *piece)], kv.at[(dst, *piece)], kvs.at[dst, j], kvr.at[dst, j], device)

    def ring_start(j):
        ring(0, 1, j, z_peer(1)).start()
        ring(0, Z - 1, j, z_peer(Z - 1)).start()

    def ring_event(level, j):
        ring(level, level, j, partner).wait_recv()

        @pl.when(level < HALF)
        def _():
            ring(level, level + 1, j, z_peer(1)).start()

        @pl.when(level < HALF)
        def _():
            ring(Z - level, Z - level, j, partner).wait_recv()

        @pl.when(level < HALF - 1)
        def _():
            ring(Z - level, Z - level - 1, j, z_peer(Z - 1)).start()

    shares = [(d, e) for d in range(Z) for e in range(2) if d or e]

    def gz_copy(d, e):
        return remote(
            gz.at[sides[e], plus_z(d)], gzr.at[e, d], gzs.at[e, d], gzrs.at[e, d], at(y, sides[e], plus_z(d))
        )

    def cz_copy(d):
        return remote(cz.at[z], cz.at[z], czs.at[d], czr.at[d], z_peer(d))

    loads = ((k_in, k), (v_in, v), (q_in, q), (ci_in, ci), (ct_in, ct), (None, None), (w_in, w))
    stores = ((x_o, x_out), (c_o, c_out), (g_o, g_out), (k_o, k_out), (v_o, v_out), (q_o, q_out))

    def load(i):
        return pltpu.make_async_copy(*loads[i], load_s.at[i])

    def store(i):
        return pltpu.make_async_copy(*stores[i], store_s.at[i])

    for i in (0, 1, 2, 3, 4, 6):
        load(i).start()
    peers = [partner, following, preceding, z_peer(1), z_peer(Z - 1)]
    peers += [y_peer(d) for d in range(1, Y)] + [head_peer(d) for d in range(1, Y)]
    barrier = pltpu.get_barrier_semaphore()
    for peer in peers:
        pl.semaphore_signal(barrier, inc=1, device_id=peer, device_id_type=MESH)
    for i in range(5):
        load(i).wait()
    kv[0, 0, pl.ds(xh, 1)] = k[:, own_cols][None]
    kv[0, 1, pl.ds(xh, 1)] = v[:, own_cols][None]
    qg[0, pl.ds(xh, 1)] = q[:, own_cols][None]
    pl.semaphore_wait(barrier, len(peers))

    for i in range(4):
        halo(i).start()
    for i in (XK, XV, XQ):
        x_copy(i).start()
    for j in range(2):
        ring_start(j)
    valid = rec[0] + rec[1] + rec[2]

    for i in (0, 1):
        halo(i).wait_recv()
    pos = ctx * ROWS - 32 + iota((ROWS + 64, WIDTH), 0)
    ext[...] = jnp.where(
        (pos >= 0) & (pos < valid), jnp.concatenate([hci[0], ci[...], hci[1]], axis=0).astype(F32), 0.0
    )
    for i in (2, 3):
        halo(i).wait_recv()
    weights = taps[...].astype(F32)
    for c in range(2):
        cols = slice(c * 128, c * 128 + 128)
        conv = jnp.zeros((ROWS + 32, 128), F32)
        for b in range(8):
            moved = ext[b : b + ROWS + 56, cols]
            for a in range(4):
                j = 8 * a + b - 1
                if 0 <= j < TAPS:
                    conv = conv + weights[j : j + 1, cols] * moved[8 * a : 8 * a + ROWS + 32]
        sig = jax.nn.sigmoid(conv)
        up = jnp.concatenate([hct[0, :, cols], ct[:, cols], hct[1, :, cols]], axis=0).astype(F32)
        slope = (up * sig * (1.0 + conv * (1.0 - sig))).astype(BF16).astype(F32)
        gpos = ctx * ROWS - 16 + iota((ROWS + 32, 128), 0)
        gex[:, cols] = jnp.where((gpos >= 0) & (gpos < N * ROWS), slope, 0.0)

    for i, j in ((XK, 2), (XV, 3)):
        x_recv(i)
        ring_start(j)
    x_recv(XQ)
    y_start(YQ)

    for c in range(2):
        cols = slice(c * 128, c * 128 + 128)
        back = jnp.zeros((ROWS, 128), F32)
        for b in range(8):
            moved = gex[b : b + ROWS + 24, cols]
            for a in range(4):
                j = TAPS - 8 * a - b
                if 0 <= j < TAPS:
                    back = back + weights[j : j + 1, cols] * moved[8 * a : 8 * a + ROWS]
        frame = ctx * ROWS + iota((ROWS, 128), 0)
        x16 = (ct[:, cols].astype(F32) + jnp.where(frame < valid, back, 0.0)).astype(BF16)
        x_o[:, cols] = x16
        xf[pl.ds(head, 1), :, cols] = x16[None]

    def head_copy(d, slot):
        return remote(xf.at[slot], xf.at[slot], head_s.at[d], head_r.at[d], head_peer(d))

    for d in range(1, Y):
        head_copy(d, head).start()
    store(0).start()
    for j in range(4):
        ring_event(1, j)

    crow = 32 // Y
    for c in range(2):
        cols = slice(c * 128, c * 128 + 128)
        grad = gex[16 : 16 + ROWS, cols]
        for b in range(8):
            moved = ext[b : b + ROWS + 40, cols]
            for a in range(2, 6):
                j = 8 * a + b - 17
                if 0 <= j < TAPS:
                    cwp[j // crow, j % crow : j % crow + 1, cols] = jnp.sum(
                        grad * moved[8 * a : 8 * a + ROWS], axis=0, keepdims=True
                    )
        cwp[Y - 1, crow - 1 : crow, cols] = jnp.zeros((1, 128), F32)
    y_start(YC1)

    y_recv(YQ)
    first_row = jnp.where(iota((16, BLOCK), 0) == 0, 1.0, 0.0).astype(BF16)
    zero_rows = jnp.zeros((112, BLOCK), BF16)
    for c in range(Y):
        cols = slice(c * BLOCK, (c + 1) * BLOCK)
        scaled = jnp.transpose(qg[c].reshape(BLOCK, PAIR).astype(F32) * (LOG2E * HEAD_DIM**-0.5))
        high = scaled.astype(BF16)
        low = (scaled - high.astype(F32)).astype(BF16)
        for h in range(2):
            rows = slice(h * HEAD_DIM, (h + 1) * HEAD_DIM)
            qta[h, :, cols] = jnp.concatenate([high[rows], low[rows], first_row, zero_rows], axis=0)

    ones_rows = jnp.ones((16, BLOCK), BF16)
    lane = iota((BLOCK, PAIR), 1)

    def prepare(slot, place):
        keys = kv[slot, 0].reshape(BLOCK, PAIR).astype(F32)
        values = kv[slot, 1].reshape(BLOCK, PAIR).astype(F32)
        kt[slot] = jnp.transpose(keys).astype(BF16)
        values_t = jnp.transpose(values).astype(BF16)
        keys_moved = pltpu.roll(keys, HEAD_DIM, 1)
        values_moved = pltpu.roll(values, HEAD_DIM, 1)
        origin = lax.rem(z + Z - slot, Z)
        row = iota((BLOCK, PAIR), 0)
        position = (y * 2 * Z + origin) * ROWS + lax.div(row, ROWS) * (Z * ROWS) + lax.rem(row, ROWS)
        bias = jnp.where((lane == 0) & (position >= valid), NEG, 0.0).astype(BF16)
        for h in range(2):
            first, second = (keys, keys_moved) if h == 0 else (keys_moved, keys)
            ka[place, h] = jnp.concatenate(
                [jnp.where(lane < HEAD_DIM, first, second).astype(BF16), bias], axis=1
            )
            mine = values if h == 0 else values_moved
            extra = jnp.where(lane < HEAD_DIM + 2, 1.0, 0.0)
            va[slot, h] = jnp.where(lane < HEAD_DIM, mine, extra).astype(BF16)
            vta[place, h] = jnp.concatenate([values_t[h * HEAD_DIM : (h + 1) * HEAD_DIM], ones_rows], axis=0)

    def forward_unit(slot, place, h):
        scores = nn(ka[place, h], qta[h])
        old = mrun[h]
        new = jnp.maximum(old, jnp.max(scores, axis=0, keepdims=True))
        p16 = jnp.exp2(scores - new).astype(BF16)
        probs[slot, h] = p16
        ot[h] = ot[h] * jnp.exp2(old - new) + nn(vta[place, h], p16)
        mrun[h] = new
        mk[slot, h] = new

    mrun[...] = jnp.full(mrun.shape, 2 * NEG, F32)
    ot[...] = jnp.zeros(ot.shape, F32)
    prepare(0, 0)
    for h in range(2):
        forward_unit(0, 0, h)

    for d in range(1, Y):
        head_copy(d, lax.rem(head + Y - d, Y)).wait_recv()
    load(6).wait()
    grad_out = jnp.zeros((ROWS, WIDTH), F32)
    for h in range(Y):
        grad_out = grad_out + nn(xf[h], w[h * WIDTH : (h + 1) * WIDTH, :])
    do_s[...] = grad_out.astype(BF16)
    for d, e in spread:
        spread_copy(SDO, d, e).start()
    dog[0, pl.ds(xh, 1)] = do_s[:, own_cols][None]
    x_copy(XF).start()

    def forward_step(d, carry):
        prepare(d, 0)

        @pl.when(d < HALF)
        def _():
            prepare(Z - d, 1)

        for j in range(4):

            @pl.when(d < HALF)
            def _():
                ring_event(d + 1, j)

            if j < 2:
                forward_unit(d, 0, j)
            else:

                @pl.when(d < HALF)
                def _():
                    forward_unit(Z - d, 1, j - 2)

        return carry

    lax.fori_loop(1, HALF + 1, forward_step, 0)

    spread_recv(SDO)
    for c in range(Y):
        cols = slice(c * BLOCK, (c + 1) * BLOCK)
        dot_[:, cols] = jnp.transpose(dog[c].reshape(BLOCK, PAIR).astype(F32))
        parts = []
        for h in range(2):
            out = ot[h, 0:HEAD_DIM, cols]
            total = ot[h, HEAD_DIM : HEAD_DIM + 1, cols]
            st[0, c, 3 * h : 3 * h + 1, :] = mrun[h, :, cols]
            st[0, c, 3 * h + 1 : 3 * h + 2, :] = total
            st[0, c, 3 * h + 2 : 3 * h + 3, :] = jnp.sum(
                out * dot_[h * HEAD_DIM : (h + 1) * HEAD_DIM, cols], axis=0, keepdims=True
            )
            parts.append(out / total)
        st[0, c, 6:8, :] = jnp.zeros((2, BLOCK), F32)
        os[c] = jnp.concatenate(parts, axis=0).astype(BF16)
    y_start(YST)
    y_start(YO)

    y_recv(YC1)
    total = cwp[y]
    for d in range(1, Y):
        total = total + cwr[d]
    c1[...] = total
    x_copy(XCW).start()
    dqt[...] = jnp.zeros(dqt.shape, F32)
    gbuf[...] = jnp.zeros(gbuf.shape, BF16)

    y_recv(YST)
    for c in range(Y):
        cols = slice(c * BLOCK, (c + 1) * BLOCK)
        rows = [st[e, (c - e) % Y] for e in range(Y)]
        for h in range(2):
            maxima = [r[3 * h : 3 * h + 1] for r in rows]
            top = functools.reduce(jnp.maximum, maxima)
            shrink = [jnp.exp2(m - top) for m in maxima]
            totals = [r[3 * h + 1 : 3 * h + 2] * f for r, f in zip(rows, shrink)]
            delta = sum(r[3 * h + 2 : 3 * h + 3] * f for r, f in zip(rows, shrink))
            inverse = 1.0 / sum(totals)
            mst[h, :, cols] = top
            lin[h, :, cols] = inverse
            dlt[h, :, cols] = delta * inverse
            if c == 0:
                for e in range(Y):
                    wts[e, h] = totals[e] * inverse

    delta_row = iota((16, Q), 0)

    def backward_unit(slot, place, parity, h):
        rows = slice(h * HEAD_DIM, (h + 1) * HEAD_DIM)
        factor = jnp.exp2(mk[slot, h] - mst[h]) * lin[h]
        shift = -dlt[h] * factor
        high = shift.astype(BF16).astype(F32)
        gbuf[h, 0:HEAD_DIM] = (dot_[rows] * factor).astype(BF16)
        gbuf[h, HEAD_DIM : HEAD_DIM + 16] = jnp.where(
            delta_row == 0, high, jnp.where(delta_row == 1, shift - high, 0.0)
        ).astype(BF16)
        slopes = nn(va[slot, h], gbuf[h])
        ds = (probs[slot, h].astype(F32) * slopes).astype(BF16)
        dsb[h] = ds
        dqt[rows] += nn(kt[slot, rows, :], ds)
        dk = nn(dsb[h], qg[...].reshape(Q, PAIR))
        part[place, parity, 0, :, rows] = dk[:, rows] * HEAD_DIM**-0.5
        part[place, parity, 1, :, rows] = nt(probs[slot, h], gbuf[h, 0:HEAD_DIM, :])

    def rs_copy(place, level, t, half, device):
        return remote(
            rss.at[place, level, t, half], rsr.at[place, level, t, half],
            rs_s.at[place, level, t, half], rs_r.at[place, level, t, half], device,
        )

    def fin_copy(kind, e, t, src):
        zz = (plus_z(1), plus_z(Z - 1), z)[kind]
        return remote(
            src, fin.at[kind, e, t], fin_s.at[kind, e, t], fin_r.at[kind, e, t], at(y, sides[e], zz)
        )

    def back_event(place, level, parity, j):
        t, half = j % 2, j // 2
        last = HALF - 1 - place
        rows = slice(half * ROWS, half * ROWS + ROWS)

        @pl.when(level > 0)
        def _():
            @pl.when(level <= last)
            def _():
                rs_copy(place, level - 1, t, half, partner).wait_recv()
                part[place, parity, t, rows] += rsr[place, level - 1, t, half].astype(F32)

        rss[place, level, t, half] = part[place, parity, t, rows].astype(BF16)

        @pl.when(level < last)
        def _():
            rs_copy(place, level, t, half, z_peer(1 if place == 0 else Z - 1)).start()

    def finish_event(place, level, kind):
        for e in range(2):
            for t in range(2):
                if kind < 2 or e == 1:
                    fin_copy(kind, e, t, rss.at[place, level, t, sides[e]]).start()

    for place in range(2):
        for h in range(2):
            backward_unit(HALF if place == 0 else HALF - 1, place, 0, h)
        for j in range(4):
            back_event(place, 0, 0, j)

    def backward_step(i, carry):
        parity = lax.rem(i, 2)
        ahead = 1 - parity

        for j in range(4):

            @pl.when(i > 0)
            def _():
                back_event(0, i, parity, j)
                back_event(1, i, parity, j)

            @pl.when(i < HALF - 1)
            def _():
                place, h = j // 2, j % 2
                backward_unit((HALF + 1 + i) if place == 0 else (HALF - 2 - i), place, ahead, h)

        @pl.when(i == HALF - 2)
        def _():
            finish_event(1, HALF - 2, 1)

        @pl.when(i == HALF - 1)
        def _():
            finish_event(1, HALF - 1, 2)
            finish_event(0, HALF - 1, 0)

        @pl.when(i == 0)
        def _():
            x_recv(XCW)
            cz[pl.ds(z, 1)] = (c1[...] + cx[...])[None]
            for d in range(1, Z):
                cz_copy(d).start()
            y_recv(YO)
            parts = []
            for h in range(2):
                rows = slice(h * HEAD_DIM, (h + 1) * HEAD_DIM)
                parts.append(
                    sum((os if e == 0 else orr)[e, rows, :].astype(F32) * wts[e, h] for e in range(Y))
                )
            attn[...] = jnp.transpose(jnp.concatenate(parts, axis=0)).astype(BF16).reshape(2, ROWS, PAIR)
            x_recv(XF)
            mine = attn[pl.ds(xh, 1)].reshape(ROWS, PAIR)
            theirs = attn[pl.ds(other, 1)].reshape(ROWS, PAIR)
            for h in range(Y):
                gs[h] = (tn(xf[h], mine) + tn(xfp[h], theirs)).astype(BF16)
            y_start(YG)

        @pl.when(i == min(2, HALF - 1))
        def _():
            y_recv(YG)
            sums = gs[pl.ds(y, 1)].reshape(WIDTH, PAIR).astype(F32)
            for d in range(1, Y):
                sums = sums + gr[d].astype(F32)
            sums = sums.reshape(2, Z, ROWS // Z, PAIR)
            gt[...] = sums
            gz[...] = sums.astype(BF16)
            for d, e in shares:
                gz_copy(d, e).start()
            for d in range(1, Z):
                slot = plus_z(Z - d)
                remote(cz.at[slot], cz.at[slot], czs.at[d], czr.at[d], partner).wait_recv()
            total = cz[0]
            for d in range(1, Z):
                total = total + cz[d]
            cfin[pl.ds(y, 1)] = total[None]
            y_start(YC2)

        return carry

    lax.fori_loop(0, HALF, backward_step, 0)

    for c in list(range(1, Y)) + [0]:
        dqs[c] = (
            jnp.transpose(dqt[:, c * BLOCK : (c + 1) * BLOCK] * HEAD_DIM**-0.5)
            .astype(BF16)
            .reshape(2, ROWS, PAIR)
        )
        for e in range(2):
            if c or e:
                spread_copy(SDQ, (Y - c) % Y, e).start()

    for d in range(1, Y):
        slot = plus_y(Y - d)
        remote(cfin.at[slot], cfin.at[slot], ys.at[YC2, d], yr.at[YC2, d], partner).wait_recv()
    for h in range(Y):
        count = min(crow, TAPS - h * crow)
        c_o[h * crow : h * crow + count, :] = cfin[h, 0:count, :]
    store(1).start()

    for d, e in shares:
        gz_copy(d, e).wait_recv()
    for e in range(2):
        sums = gt[pl.ds(xh, 1), pl.ds(z, 1)].reshape(ROWS // Z, PAIR) if e == 0 else gzr[1, 0].astype(F32)
        for d in range(1, Z):
            sums = sums + gzr[e, d].astype(F32)
        g_o[:, side_cols[e]] = sums
    store(2).start()

    for t, out in ((0, k_o), (1, v_o)):
        for e in range(2):
            for kind in range(3):
                if kind < 2 or e == 1:
                    fin_copy(kind, e, t, fin.at[kind, e, t]).wait_recv()
            total = fin[0, e, t].astype(F32) + fin[1, e, t].astype(F32)
            if e == 0:
                start = pl.multiple_of(xh * ROWS, ROWS)
                total = total + part[1, (HALF - 1) % 2, t, pl.ds(start, ROWS), :]
            else:
                total = total + fin[2, 1, t].astype(F32)
            out[:, side_cols[e]] = total.astype(BF16)
        store(3 + t).start()

    spread_recv(SDQ)
    for e in range(2):
        total = dqs[0, pl.ds(xh, 1)].reshape(ROWS, PAIR).astype(F32) if e == 0 else dqr[0, 1].astype(F32)
        for d in range(1, Y):
            total = total + dqr[d, e].astype(F32)
        q_o[:, side_cols[e]] = total.astype(BF16)
    store(5).start()

    for i in range(4):
        halo(i).wait_send()
    for i in range(5):
        x_copy(i).wait_send()
    for i in range(6):
        for d in range(1, Y):
            y_copy(i, d).wait_send()
    for i in range(2):
        for d, e in spread:
            spread_copy(i, d, e).wait_send()
    for d in range(1, Y):
        head_copy(d, head).wait_send()
    for slot in range(1, Z):
        for j in range(4):
            ring(slot, slot, j, partner).wait_send()
    for t in range(2):
        for half in range(2):
            for level in range(HALF - 1):
                rs_copy(0, level, t, half, partner).wait_send()
            for level in range(HALF - 2):
                rs_copy(1, level, t, half, partner).wait_send()
        for e in range(2):
            for kind in range(3):
                if kind < 2 or e == 1:
                    fin_copy(kind, e, t, fin.at[kind, e, t]).wait_send()
    for d, e in shares:
        gz_copy(d, e).wait_send()
    for d in range(1, Z):
        cz_copy(d).wait_send()
    for i in range(6):
        store(i).wait()


def store_kernel(*refs):
    half = len(refs) // 2
    for source, target in zip(refs[:half], refs[half:]):
        target[...] = source[...]


def on_device(Y, Z, query_all, key_all, value_all, cotangent, conv_input, rec_lengths, out_proj, conv_weight):
    Q = Y * BLOCK
    vm, dma = pltpu.VMEM, pltpu.SemaphoreType.DMA
    vmem = pl.BlockSpec(memory_space=pltpu.VMEM)
    crow = 32 // Y
    block = (ROWS, WIDTH)
    anywhere = pl.BlockSpec(memory_space=pl.ANY)
    scratch = [vm(block, BF16) for name in ("q", "k", "v", "ct", "ci")]
    scratch += [vm((Y * WIDTH, WIDTH), BF16)]
    scratch += [vm(block, BF16) for name in ("q_o", "k_o", "v_o", "x_o")]
    scratch += [
        vm((ROWS // Z, WIDTH), F32),
        vm((TAPS, WIDTH), F32),
        dma((7,)),
        dma((6,)),
        vm((Z, 2, 2, ROWS, PAIR), BF16),
        vm((Y, 2, ROWS, PAIR), BF16),
        vm((Y, 2, ROWS, PAIR), BF16),
        vm((Z, PAIR, BLOCK), BF16),
        vm((Z, 2, BLOCK, PAIR), BF16),
        vm((2, 2, BLOCK, 2 * PAIR), BF16),
        vm((2, 2, HEAD_DIM + 16, BLOCK), BF16),
        vm((2, 2 * PAIR, Q), BF16),
        vm((Z, 2, BLOCK, Q), BF16),
        vm((Z, 2, 1, Q), F32),
        vm((2, 1, Q), F32),
        vm((2, HEAD_DIM + 16, Q), F32),
        vm((PAIR, Q), F32),
        vm((PAIR, Q), F32),
        vm((2, 1, Q), F32),
        vm((2, 1, Q), F32),
        vm((2, 1, Q), F32),
        vm((Y, 2, 1, BLOCK), F32),
        vm((2, PAIR, Q), BF16),
        vm((2, BLOCK, Q), BF16),
        vm((2, 32, WIDTH), BF16),
        vm((2, 16, WIDTH), BF16),
        vm((ROWS + 64, WIDTH), F32),
        vm((ROWS + 32, WIDTH), F32),
        vm((Y, ROWS, WIDTH), BF16),
        vm((Y, ROWS, WIDTH), BF16),
        vm(block, BF16),
        vm((Y, Y, 8, BLOCK), F32),
        vm((Y, PAIR, BLOCK), BF16),
        vm((Y, PAIR, BLOCK), BF16),
        vm((2, ROWS, PAIR), BF16),
        vm((Y, WIDTH, PAIR), BF16),
        vm((Y, WIDTH, PAIR), BF16),
        vm((2, Z, ROWS // Z, PAIR), F32),
        vm((2, Z, ROWS // Z, PAIR), BF16),
        vm((2, Z, ROWS // Z, PAIR), BF16),
        vm((2, 2, 2, BLOCK, PAIR), F32),
        vm((2, Z // 2, 2, 2, ROWS, PAIR), BF16),
        vm((2, Z // 2, 2, 2, ROWS, PAIR), BF16),
        vm((3, 2, 2, ROWS, PAIR), BF16),
        vm((Y, 2, ROWS, PAIR), BF16),
        vm((Y, 2, ROWS, PAIR), BF16),
        vm((Y, crow, WIDTH), F32),
        vm((Y, crow, WIDTH), F32),
        vm((crow, WIDTH), F32),
        vm((crow, WIDTH), F32),
        vm((Z, crow, WIDTH), F32),
        vm((Y, crow, WIDTH), F32),
    ]
    semaphores = [
        (4,),
        (Y,),
        (5,),
        (6, Y),
        (2, Y, 2),
        (Z, 4),
        (2, Z // 2, 2, 2),
        (3, 2, 2),
        (2, Z),
        (Z,),
    ]
    for shape in semaphores:
        scratch += [dma(shape), dma(shape)]
    shapes = (
        jax.ShapeDtypeStruct(block, BF16),
        jax.ShapeDtypeStruct(block, BF16),
        jax.ShapeDtypeStruct(block, BF16),
        jax.ShapeDtypeStruct(block, BF16),
        jax.ShapeDtypeStruct((ROWS // Z, WIDTH), F32),
        jax.ShapeDtypeStruct((TAPS, WIDTH), F32),
    )
    results = pl.pallas_call(
        functools.partial(fused_kernel, Y, Z),
        out_shape=shapes,
        in_specs=[pl.BlockSpec(memory_space=pltpu.SMEM)] + [anywhere] * 6 + [vmem],
        out_specs=(anywhere,) * 6,
        scratch_shapes=scratch,
        compiler_params=pltpu.CompilerParams(
            collective_id=0, has_side_effects=True, vmem_limit_bytes=56 * 1024 * 1024
        ),
        name="conv_attention_backward",
    )(rec_lengths, query_all, key_all, value_all, cotangent, conv_input, out_proj, conv_weight)
    return pl.pallas_call(
        store_kernel, out_shape=shapes, in_specs=[vmem] * 6, out_specs=(vmem,) * 6, name="store_results"
    )(*results)


def solution(mesh):
    sizes = dict(mesh.shape)
    Y = sizes["head"]
    Z = sizes["ctx"] // (2 * Y)
    both = P("ctx", "head")
    return jax.shard_map(
        functools.partial(on_device, Y, Z),
        mesh=mesh,
        in_specs=(both, both, both, both, both, P(), P(None, "head"), P(None, "head")),
        out_specs=(both, both, both, both, both, P(None, "head")),
        check_vma=False,
    )
```

time: 92.1 us -> 69.1 us (0.75); the launches traced: 90.3 us -> 68.9 us
  Pallas kernels: 84.3 us -> 68.2 us
  local copies, waits for them, and re-layouts: 5.33 us -> 0 us
    pallas_call x1 -> x2, Pallas kernels: 84.3 us -> 68.2 us  [the longest x1 66.6 us: on_device(): pl.pallas_call(functools.partial(fused_kernel, Y, Z), out_shape=shapes, i...]
    unnamed x16 -> x0, local copies, waits for them, and re-layouts: 5.33 us -> none
where the time goes in v2:
time: 69.1 us; the launch traced here: 68.9 us
  Pallas kernels  68.2 us (99%)
    pallas_call x1, Pallas kernels, on_device(): pl.pallas_call(functools.partial(fused_kernel, Y, Z), out_shape=shapes, i...  66.6 us
    pallas_call x1, Pallas kernels, on_device(): pl.pallas_call(store_kernel, out_shape=shapes, in_specs=[vmem] * 6, out_s...  1.65 us

profile of v2, /device:TPU:2, one launch (start us, length us, event | category | flops | bytes accessed | tf_op | source)
XLA Modules:
  0.0 68.9 jit_solution(6304654587965419534)
XLA Ops:
  0.6 66.6 %conv_attention_backward.1 = (bf16[128,256]{1,0:T(8,128)(2,1)}, bf16[128,256]{1,0:T(8,128)(2,1)}, bf16[128,256]{1,0:T(8,128)(2,1)}, bf16[128,256]{1,0:T(8,128)(2...) custom-call(s32[3]{0:T(128)} %rec.1, bf16[128,256]{1,0:T(8,128)(2,1)} %q_in.1, bf16[128,256]{1,0:T(8,128)(2,1)} %k_in.1, ...), custom_call_target="tpu_custom_call" | custom-call | tf_op jit(solution)/shard_map/conv_attention_backward/pallas_call | solution.py:727
  67.2 1.7 %store_results.1 = (bf16[128,256]{1,0:T(8,128)(2,1)}, bf16[128,256]{1,0:T(8,128)(2,1)}, bf16[128,256]{1,0:T(8,128)(2,1)}, bf16[128,256]{1,0:T(8,128)(2,1)}, f32[16,256]{1,0:T(8,128)}, /*index=5*/f32[31,256]{1,0:T(8,128)}) custom-call(bf16[128,256]{1,0:T(8,128)(2,1)} %get-tuple-element.12.refs_0_, bf16[128,256]{1,0:T(8,128)(2,1)} %get-tuple-element.13.refs_1_, ...), custom_call_target="tpu_custom_call" | custom-call | tf_op jit(solution)/shard_map/store_results/pallas_call | solution.py:738

commit v3 on v2

--- a/solution.py
+++ b/solution.py
@@ -97,13 +97,12 @@
         )[i]
         return remote(src, dst, halo_s.at[i], halo_r.at[i], dev)
 
-    XK, XV, XQ, XF, XCW = range(5)
+    XK, XV, XF, XCW = range(4)
 
     def x_copy(i):
         src, dst = (
             lambda: (k.at[:, other_cols], kv.at[0, 0, xh]),
             lambda: (v.at[:, other_cols], kv.at[0, 1, xh]),
-            lambda: (q.at[:, other_cols], qg.at[0, xh]),
             lambda: (xf, xfp),
             lambda: (c1, cx),
         )[i]()
@@ -111,16 +110,15 @@
 
     def x_recv(i):
         if i < XF:
-            dst = (kv.at[0, 0, other], kv.at[0, 1, other], qg.at[0, other])[i]
+            dst = kv.at[0, i, other]
             remote(dst, dst, xs.at[i], xr.at[i], partner).wait_recv()
         else:
             x_copy(i).wait_recv()
 
-    YQ, YST, YO, YG, YC1, YC2 = range(6)
+    YST, YO, YG, YC1, YC2 = range(5)
 
     def y_copy(i, d):
         src, dst = (
-            lambda: (qg.at[0], qg.at[d]),
             lambda: (st.at[0], st.at[d]),
             lambda: (os.at[Y - d], orr.at[d]),
             lambda: (gs.at[plus_y(d)], gr.at[d]),
@@ -138,18 +136,20 @@
             y_copy(i, d).wait_recv()
 
     spread = [(d, e) for d in range(Y) for e in range(2) if d or e]
-    SDO, SDQ = range(2)
+    spread.sort(key=lambda pair: -min(pair[0], Y - pair[0]) - 2 * pair[1])
+    SDO, SDQ, SQ = range(3)
 
     def spread_copy(i, d, e):
         src, dst = (
             lambda: (do_s.at[:, side_cols[e]], dog.at[d, xh]),
             lambda: (dqs.at[(Y - d) % Y, sides[e]], dqr.at[d, e]),
+            lambda: (q.at[:, side_cols[e]], qg.at[d, xh]),
         )[i]()
         return remote(src, dst, yxs.at[i, d, e], yxr.at[i, d, e], at(plus_y(d), sides[e], z))
 
     def spread_recv(i):
         for d, e in spread:
-            dst = dog.at[d, sides[e]] if i == SDO else dqr.at[d, e]
+            dst = (dog.at[d, sides[e]], dqr.at[d, e], qg.at[d, sides[e]])[i]
             remote(dst, dst, yxs.at[i, d, e], yxr.at[i, d, e], partner).wait_recv()
 
     def ring(src, dst, j, device):
@@ -197,7 +197,8 @@
     for i in (0, 1, 2, 3, 4, 6):
         load(i).start()
     peers = [partner, following, preceding, z_peer(1), z_peer(Z - 1)]
-    peers += [y_peer(d) for d in range(1, Y)] + [head_peer(d) for d in range(1, Y)]
+    peers += [at(plus_y(d), side, z) for d in range(1, Y) for side in sides]
+    peers += [head_peer(d) for d in range(1, Y)]
     barrier = pltpu.get_barrier_semaphore()
     for peer in peers:
         pl.semaphore_signal(barrier, inc=1, device_id=peer, device_id_type=MESH)
@@ -210,10 +211,12 @@
 
     for i in range(4):
         halo(i).start()
-    for i in (XK, XV, XQ):
+    for i in (XK, XV):
         x_copy(i).start()
     for j in range(2):
         ring_start(j)
+    for d, e in spread:
+        spread_copy(SQ, d, e).start()
     valid = rec[0] + rec[1] + rec[2]
 
     for i in (0, 1):
@@ -243,8 +246,6 @@
     for i, j in ((XK, 2), (XV, 3)):
         x_recv(i)
         ring_start(j)
-    x_recv(XQ)
-    y_start(YQ)
 
     for c in range(2):
         cols = slice(c * 128, c * 128 + 128)
@@ -263,11 +264,58 @@
     def head_copy(d, slot):
         return remote(xf.at[slot], xf.at[slot], head_s.at[d], head_r.at[d], head_peer(d))
 
-    for d in range(1, Y):
+    for d in [2, 1, 3] if Y == 4 else range(1, Y):
         head_copy(d, head).start()
     store(0).start()
     for j in range(4):
         ring_event(1, j)
+
+    spread_recv(SQ)
+    first_row = jnp.where(iota((16, BLOCK), 0) == 0, 1.0, 0.0).astype(BF16)
+    zero_rows = jnp.zeros((112, BLOCK), BF16)
+    for c in range(Y):
+        cols = slice(c * BLOCK, (c + 1) * BLOCK)
+        scaled = jnp.transpose(qg[c].reshape(BLOCK, PAIR).astype(F32) * (LOG2E * HEAD_DIM**-0.5))
+        high = scaled.astype(BF16)
+        low = (scaled - high.astype(F32)).astype(BF16)
+        for h in range(2):
+            rows = slice(h * HEAD_DIM, (h + 1) * HEAD_DIM)
+            qta[h, :, cols] = jnp.concatenate([high[rows], low[rows], first_row, zero_rows], axis=0)
+
+    ones_rows = jnp.ones((16, BLOCK), BF16)
+    lane = iota((BLOCK, PAIR), 1)
+
+    def prepare(slot, place):
+        keys = kv[slot, 0].reshape(BLOCK, PAIR).astype(F32)
+        values = kv[slot, 1].reshape(BLOCK, PAIR).astype(F32)
+        values_t = jnp.transpose(values).astype(BF16)
+        keys_moved = pltpu.roll(keys, HEAD_DIM, 1)
+        origin = lax.rem(z + Z - slot, Z)
+        row = iota((BLOCK, PAIR), 0)
+        position = (y * 2 * Z + origin) * ROWS + lax.div(row, ROWS) * (Z * ROWS) + lax.rem(row, ROWS)
+        bias = jnp.where((lane == 0) & (position >= valid), NEG, 0.0).astype(BF16)
+        for h in range(2):
+            first, second = (keys, keys_moved) if h == 0 else (keys_moved, keys)
+            ka[place, h] = jnp.concatenate(
+                [jnp.where(lane < HEAD_DIM, first, second).astype(BF16), bias], axis=1
+            )
+            vta[place, h] = jnp.concatenate([values_t[h * HEAD_DIM : (h + 1) * HEAD_DIM], ones_rows], axis=0)
+
+    def forward_unit(slot, place, h):
+        scores = nn(ka[place, h], qta[h])
+        old = mrun[h]
+        new = jnp.maximum(old, jnp.max(scores, axis=0, keepdims=True))
+        p16 = jnp.exp2(scores - new).astype(BF16)
+        probs[slot, h] = p16
+        ot[h] = ot[h] * jnp.exp2(old - new) + nn(vta[place, h], p16)
+        mrun[h] = new
+        mk[slot, h] = new
+
+    mrun[...] = jnp.full(mrun.shape, 2 * NEG, F32)
+    ot[...] = jnp.zeros(ot.shape, F32)
+    prepare(0, 0)
+    for h in range(2):
+        forward_unit(0, 0, h)
 
     crow = 32 // Y
     for c in range(2):
@@ -284,58 +332,6 @@
         cwp[Y - 1, crow - 1 : crow, cols] = jnp.zeros((1, 128), F32)
     y_start(YC1)
 
-    y_recv(YQ)
-    first_row = jnp.where(iota((16, BLOCK), 0) == 0, 1.0, 0.0).astype(BF16)
-    zero_rows = jnp.zeros((112, BLOCK), BF16)
-    for c in range(Y):
-        cols = slice(c * BLOCK, (c + 1) * BLOCK)
-        scaled = jnp.transpose(qg[c].reshape(BLOCK, PAIR).astype(F32) * (LOG2E * HEAD_DIM**-0.5))
-        high = scaled.astype(BF16)
-        low = (scaled - high.astype(F32)).astype(BF16)
-        for h in range(2):
-            rows = slice(h * HEAD_DIM, (h + 1) * HEAD_DIM)
-            qta[h, :, cols] = jnp.concatenate([high[rows], low[rows], first_row, zero_rows], axis=0)
-
-    ones_rows = jnp.ones((16, BLOCK), BF16)
-    lane = iota((BLOCK, PAIR), 1)
-
-    def prepare(slot, place):
-        keys = kv[slot, 0].reshape(BLOCK, PAIR).astype(F32)
-        values = kv[slot, 1].reshape(BLOCK, PAIR).astype(F32)
-        kt[slot] = jnp.transpose(keys).astype(BF16)
-        values_t = jnp.transpose(values).astype(BF16)
-        keys_moved = pltpu.roll(keys, HEAD_DIM, 1)
-        values_moved = pltpu.roll(values, HEAD_DIM, 1)
-        origin = lax.rem(z + Z - slot, Z)
-        row = iota((BLOCK, PAIR), 0)
-        position = (y * 2 * Z + origin) * ROWS + lax.div(row, ROWS) * (Z * ROWS) + lax.rem(row, ROWS)
-        bias = jnp.where((lane == 0) & (position >= valid), NEG, 0.0).astype(BF16)
-        for h in range(2):
-            first, second = (keys, keys_moved) if h == 0 else (keys_moved, keys)
-            ka[place, h] = jnp.concatenate(
-                [jnp.where(lane < HEAD_DIM, first, second).astype(BF16), bias], axis=1
-            )
-            mine = values if h == 0 else values_moved
-            extra = jnp.where(lane < HEAD_DIM + 2, 1.0, 0.0)
-            va[slot, h] = jnp.where(lane < HEAD_DIM, mine, extra).astype(BF16)
-            vta[place, h] = jnp.concatenate([values_t[h * HEAD_DIM : (h + 1) * HEAD_DIM], ones_rows], axis=0)
-
-    def forward_unit(slot, place, h):
-        scores = nn(ka[place, h], qta[h])
-        old = mrun[h]
-        new = jnp.maximum(old, jnp.max(scores, axis=0, keepdims=True))
-        p16 = jnp.exp2(scores - new).astype(BF16)
-        probs[slot, h] = p16
-        ot[h] = ot[h] * jnp.exp2(old - new) + nn(vta[place, h], p16)
-        mrun[h] = new
-        mk[slot, h] = new
-
-    mrun[...] = jnp.full(mrun.shape, 2 * NEG, F32)
-    ot[...] = jnp.zeros(ot.shape, F32)
-    prepare(0, 0)
-    for h in range(2):
-        forward_unit(0, 0, h)
-
     for d in range(1, Y):
         head_copy(d, lax.rem(head + Y - d, Y)).wait_recv()
     load(6).wait()
@@ -377,7 +373,6 @@
     for c in range(Y):
         cols = slice(c * BLOCK, (c + 1) * BLOCK)
         dot_[:, cols] = jnp.transpose(dog[c].reshape(BLOCK, PAIR).astype(F32))
-        parts = []
         for h in range(2):
             out = ot[h, 0:HEAD_DIM, cols]
             total = ot[h, HEAD_DIM : HEAD_DIM + 1, cols]
@@ -386,11 +381,16 @@
             st[0, c, 3 * h + 2 : 3 * h + 3, :] = jnp.sum(
                 out * dot_[h * HEAD_DIM : (h + 1) * HEAD_DIM, cols], axis=0, keepdims=True
             )
-            parts.append(out / total)
         st[0, c, 6:8, :] = jnp.zeros((2, BLOCK), F32)
+    y_start(YST)
+    for c in list(range(1, Y)) + [0]:
+        cols = slice(c * BLOCK, (c + 1) * BLOCK)
+        parts = [
+            ot[h, 0:HEAD_DIM, cols] * (1.0 / ot[h, HEAD_DIM : HEAD_DIM + 1, cols]) for h in range(2)
+        ]
         os[c] = jnp.concatenate(parts, axis=0).astype(BF16)
-    y_start(YST)
-    y_start(YO)
+        if c:
+            y_copy(YO, Y - c).start()
 
     y_recv(YC1)
     total = cwp[y]
@@ -399,6 +399,16 @@
     c1[...] = total
     x_copy(XCW).start()
     dqt[...] = jnp.zeros(dqt.shape, F32)
+
+    def arrange(slot, carry):
+        values = kv[slot, 1].reshape(BLOCK, PAIR).astype(F32)
+        kt[slot] = jnp.transpose(kv[slot, 0].reshape(BLOCK, PAIR).astype(F32)).astype(BF16)
+        extra = jnp.where(lane < HEAD_DIM + 2, 1.0, 0.0)
+        for h, mine in enumerate((values, pltpu.roll(values, HEAD_DIM, 1))):
+            va[slot, h] = jnp.where(lane < HEAD_DIM, mine, extra).astype(BF16)
+        return carry
+
+    lax.fori_loop(0, Z, arrange, 0)
     gbuf[...] = jnp.zeros(gbuf.shape, BF16)
 
     y_recv(YST)
@@ -499,6 +509,15 @@
         @pl.when(i == HALF - 2)
         def _():
             finish_event(1, HALF - 2, 1)
+            for c in sorted(range(Y), key=lambda c: -min(c, Y - c)):
+                dqs[c] = (
+                    jnp.transpose(dqt[:, c * BLOCK : (c + 1) * BLOCK] * HEAD_DIM**-0.5)
+                    .astype(BF16)
+                    .reshape(2, ROWS, PAIR)
+                )
+                for e in (1, 0):
+                    if c or e:
+                        spread_copy(SDQ, (Y - c) % Y, e).start()
 
         @pl.when(i == HALF - 1)
         def _():
@@ -550,16 +569,6 @@
 
     lax.fori_loop(0, HALF, backward_step, 0)
 
-    for c in list(range(1, Y)) + [0]:
-        dqs[c] = (
-            jnp.transpose(dqt[:, c * BLOCK : (c + 1) * BLOCK] * HEAD_DIM**-0.5)
-            .astype(BF16)
-            .reshape(2, ROWS, PAIR)
-        )
-        for e in range(2):
-            if c or e:
-                spread_copy(SDQ, (Y - c) % Y, e).start()
-
     for d in range(1, Y):
         slot = plus_y(Y - d)
         remote(cfin.at[slot], cfin.at[slot], ys.at[YC2, d], yr.at[YC2, d], partner).wait_recv()
@@ -601,12 +610,12 @@
 
     for i in range(4):
         halo(i).wait_send()
+    for i in range(4):
+        x_copy(i).wait_send()
     for i in range(5):
-        x_copy(i).wait_send()
-    for i in range(6):
         for d in range(1, Y):
             y_copy(i, d).wait_send()
-    for i in range(2):
+    for i in range(3):
         for d, e in spread:
             spread_copy(i, d, e).wait_send()
     for d in range(1, Y):
@@ -705,9 +714,9 @@
     semaphores = [
         (4,),
         (Y,),
-        (5,),
-        (6, Y),
-        (2, Y, 2),
+        (4,),
+        (5, Y),
+        (3, Y, 2),
         (Z, 4),
         (2, Z // 2, 2, 2),
         (3, 2, 2),

time: 69.1 us -> 67.4 us (0.975)
  Pallas kernels: 68.2 us -> 66.1 us
    pallas_call x1, Pallas kernels: 66.6 us -> 64.4 us  [on_device(): pl.pallas_call(functools.partial(fused_kernel, Y, Z), out_shape=shapes, i...]
where the time goes in v3:
time: 67.4 us; the launch traced here: 66.7 us
  Pallas kernels  66.1 us (98%)
    pallas_call x1, Pallas kernels, on_device(): pl.pallas_call(functools.partial(fused_kernel, Y, Z), out_shape=shapes, i...  64.4 us
    pallas_call x1, Pallas kernels, on_device(): pl.pallas_call(store_kernel, out_shape=shapes, in_specs=[vmem] * 6, out_s...  1.65 us

profile of v3, /device:TPU:2, one launch (start us, length us, event | category | flops | bytes accessed | tf_op | source)
XLA Modules:
  0.0 66.7 jit_solution(13760853363568550454)
XLA Ops:
  0.6 64.4 %conv_attention_backward.1 = (bf16[128,256]{1,0:T(8,128)(2,1)}, bf16[128,256]{1,0:T(8,128)(2,1)}, bf16[128,256]{1,0:T(8,128)(2,1)}, bf16[128,256]{1,0:T(8,128)(2...) custom-call(s32[3]{0:T(128)} %rec.1, bf16[128,256]{1,0:T(8,128)(2,1)} %q_in.1, bf16[128,256]{1,0:T(8,128)(2,1)} %k_in.1, ...), custom_call_target="tpu_custom_call" | custom-call | tf_op jit(solution)/shard_map/conv_attention_backward/pallas_call | solution.py:736
  65.1 1.7 %store_results.1 = (bf16[128,256]{1,0:T(8,128)(2,1)}, bf16[128,256]{1,0:T(8,128)(2,1)}, bf16[128,256]{1,0:T(8,128)(2,1)}, bf16[128,256]{1,0:T(8,128)(2,1)}, f32[16,256]{1,0:T(8,128)}, /*index=5*/f32[31,256]{1,0:T(8,128)}) custom-call(bf16[128,256]{1,0:T(8,128)(2,1)} %get-tuple-element.12.refs_0_, bf16[128,256]{1,0:T(8,128)(2,1)} %get-tuple-element.13.refs_1_, ...), custom_call_target="tpu_custom_call" | custom-call | tf_op jit(solution)/shard_map/store_results/pallas_call | solution.py:747

commit v4 on v3

--- a/solution.py
+++ b/solution.py
@@ -455,34 +455,33 @@
         )
 
     def fin_copy(kind, e, t, src):
-        zz = (plus_z(1), plus_z(Z - 1), z)[kind]
+        zz = (plus_z(1), z)[kind]
         return remote(
             src, fin.at[kind, e, t], fin_s.at[kind, e, t], fin_r.at[kind, e, t], at(y, sides[e], zz)
         )
 
     def back_event(place, level, parity, j):
-        t, half = j % 2, j // 2
-        last = HALF - 1 - place
-        rows = slice(half * ROWS, half * ROWS + ROWS)
+        t, e = j % 2, 1 - j // 2
+        half = sides[e]
+        last = HALF - 1
+        rows = pl.ds(pl.multiple_of(half * ROWS, ROWS), ROWS)
 
         @pl.when(level > 0)
         def _():
-            @pl.when(level <= last)
+            rs_copy(place, level - 1, t, half, partner).wait_recv()
+            part[place, parity, t, rows] += rsr[place, level - 1, t, half].astype(F32)
+
+        rss[place, level, t, half] = part[place, parity, t, rows].astype(BF16)
+
+        @pl.when(level < last)
+        def _():
+            rs_copy(place, level, t, half, z_peer(1 if place == 0 else Z - 1)).start()
+
+        if place == 0 or e == 1:
+
+            @pl.when(level == last)
             def _():
-                rs_copy(place, level - 1, t, half, partner).wait_recv()
-                part[place, parity, t, rows] += rsr[place, level - 1, t, half].astype(F32)
-
-        rss[place, level, t, half] = part[place, parity, t, rows].astype(BF16)
-
-        @pl.when(level < last)
-        def _():
-            rs_copy(place, level, t, half, z_peer(1 if place == 0 else Z - 1)).start()
-
-    def finish_event(place, level, kind):
-        for e in range(2):
-            for t in range(2):
-                if kind < 2 or e == 1:
-                    fin_copy(kind, e, t, rss.at[place, level, t, sides[e]]).start()
+                fin_copy(place, e, t, rss.at[place, level, t, half]).start()
 
     for place in range(2):
         for h in range(2):
@@ -508,7 +507,6 @@
 
         @pl.when(i == HALF - 2)
         def _():
-            finish_event(1, HALF - 2, 1)
             for c in sorted(range(Y), key=lambda c: -min(c, Y - c)):
                 dqs[c] = (
                     jnp.transpose(dqt[:, c * BLOCK : (c + 1) * BLOCK] * HEAD_DIM**-0.5)
@@ -518,11 +516,6 @@
                 for e in (1, 0):
                     if c or e:
                         spread_copy(SDQ, (Y - c) % Y, e).start()
-
-        @pl.when(i == HALF - 1)
-        def _():
-            finish_event(1, HALF - 1, 2)
-            finish_event(0, HALF - 1, 0)
 
         @pl.when(i == 0)
         def _():
@@ -588,15 +581,14 @@
 
     for t, out in ((0, k_o), (1, v_o)):
         for e in range(2):
-            for kind in range(3):
-                if kind < 2 or e == 1:
-                    fin_copy(kind, e, t, fin.at[kind, e, t]).wait_recv()
-            total = fin[0, e, t].astype(F32) + fin[1, e, t].astype(F32)
+            for kind in range(1 + e):
+                fin_copy(kind, e, t, fin.at[kind, e, t]).wait_recv()
+            total = fin[0, e, t].astype(F32)
             if e == 0:
                 start = pl.multiple_of(xh * ROWS, ROWS)
                 total = total + part[1, (HALF - 1) % 2, t, pl.ds(start, ROWS), :]
             else:
-                total = total + fin[2, 1, t].astype(F32)
+                total = total + fin[1, 1, t].astype(F32)
             out[:, side_cols[e]] = total.astype(BF16)
         store(3 + t).start()
 
@@ -626,13 +618,11 @@
     for t in range(2):
         for half in range(2):
             for level in range(HALF - 1):
-                rs_copy(0, level, t, half, partner).wait_send()
-            for level in range(HALF - 2):
-                rs_copy(1, level, t, half, partner).wait_send()
+                for place in range(2):
+                    rs_copy(place, level, t, half, partner).wait_send()
         for e in range(2):
-            for kind in range(3):
-                if kind < 2 or e == 1:
-                    fin_copy(kind, e, t, fin.at[kind, e, t]).wait_send()
+            for kind in range(1 + e):
+                fin_copy(kind, e, t, fin.at[kind, e, t]).wait_send()
     for d, e in shares:
         gz_copy(d, e).wait_send()
     for d in range(1, Z):
@@ -701,7 +691,7 @@
         vm((2, 2, 2, BLOCK, PAIR), F32),
         vm((2, Z // 2, 2, 2, ROWS, PAIR), BF16),
         vm((2, Z // 2, 2, 2, ROWS, PAIR), BF16),
-        vm((3, 2, 2, ROWS, PAIR), BF16),
+        vm((2, 2, 2, ROWS, PAIR), BF16),
         vm((Y, 2, ROWS, PAIR), BF16),
         vm((Y, 2, ROWS, PAIR), BF16),
         vm((Y, crow, WIDTH), F32),
@@ -719,7 +709,7 @@
         (3, Y, 2),
         (Z, 4),
         (2, Z // 2, 2, 2),
-        (3, 2, 2),
+        (2, 2, 2),
         (2, Z),
         (Z,),
     ]

time: 67.4 us -> 65.7 us (0.975)
  Pallas kernels: 66.1 us -> 64.8 us
    pallas_call x1, Pallas kernels: 64.4 us -> 63.1 us  [on_device(): pl.pallas_call(functools.partial(fused_kernel, Y, Z), out_shape=shapes, i...]
where the time goes in v4:
time: 65.7 us; the launch traced here: 65.4 us
  Pallas kernels  64.8 us (99%)
    pallas_call x1, Pallas kernels, on_device(): pl.pallas_call(functools.partial(fused_kernel, Y, Z), out_shape=shapes, i...  63.1 us
    pallas_call x1, Pallas kernels, on_device(): pl.pallas_call(store_kernel, out_shape=shapes, in_specs=[vmem] * 6, out_s...  1.65 us

profile of v4, /device:TPU:2, one launch (start us, length us, event | category | flops | bytes accessed | tf_op | source)
XLA Modules:
  0.0 65.4 jit_solution(7798874511542464550)
XLA Ops:
  0.6 63.1 %conv_attention_backward.1 = (bf16[128,256]{1,0:T(8,128)(2,1)}, bf16[128,256]{1,0:T(8,128)(2,1)}, bf16[128,256]{1,0:T(8,128)(2,1)}, bf16[128,256]{1,0:T(8,128)(2...) custom-call(s32[3]{0:T(128)} %rec.1, bf16[128,256]{1,0:T(8,128)(2,1)} %q_in.1, bf16[128,256]{1,0:T(8,128)(2,1)} %k_in.1, ...), custom_call_target="tpu_custom_call" | custom-call | tf_op jit(solution)/shard_map/conv_attention_backward/pallas_call | solution.py:726
  63.8 1.7 %store_results.1 = (bf16[128,256]{1,0:T(8,128)(2,1)}, bf16[128,256]{1,0:T(8,128)(2,1)}, bf16[128,256]{1,0:T(8,128)(2,1)}, bf16[128,256]{1,0:T(8,128)(2,1)}, f32[16,256]{1,0:T(8,128)}, /*index=5*/f32[31,256]{1,0:T(8,128)}) custom-call(bf16[128,256]{1,0:T(8,128)(2,1)} %get-tuple-element.12.refs_0_, bf16[128,256]{1,0:T(8,128)(2,1)} %get-tuple-element.13.refs_1_, ...), custom_call_target="tpu_custom_call" | custom-call | tf_op jit(solution)/shard_map/store_results/pallas_call | solution.py:737

commit v5 on v4

--- a/solution.py
+++ b/solution.py
@@ -497,8 +497,9 @@
 
             @pl.when(i > 0)
             def _():
-                back_event(0, i, parity, j)
-                back_event(1, i, parity, j)
+                for piece in ((0, 1), (2, 3), (), ())[j]:
+                    back_event(0, i, parity, piece)
+                    back_event(1, i, parity, piece)
 
             @pl.when(i < HALF - 1)
             def _():

time: 65.7 us -> 66.2 us (level)
  no operation moved by 1% of the time
where the time goes in v5:
time: 66.2 us; the launch traced here: 65.9 us
  Pallas kernels  65.3 us (99%)
    pallas_call x1, Pallas kernels, on_device(): pl.pallas_call(functools.partial(fused_kernel, Y, Z), out_shape=shapes, i...  63.6 us
    pallas_call x1, Pallas kernels, on_device(): pl.pallas_call(store_kernel, out_shape=shapes, in_specs=[vmem] * 6, out_s...  1.65 us

profile of v5, /device:TPU:2, one launch (start us, length us, event | category | flops | bytes accessed | tf_op | source)
XLA Modules:
  0.0 65.9 jit_solution(1753609972916606051)
XLA Ops:
  0.6 63.6 %conv_attention_backward.1 = (bf16[128,256]{1,0:T(8,128)(2,1)}, bf16[128,256]{1,0:T(8,128)(2,1)}, bf16[128,256]{1,0:T(8,128)(2,1)}, bf16[128,256]{1,0:T(8,128)(2...) custom-call(s32[3]{0:T(128)} %rec.1, bf16[128,256]{1,0:T(8,128)(2,1)} %q_in.1, bf16[128,256]{1,0:T(8,128)(2,1)} %k_in.1, ...), custom_call_target="tpu_custom_call" | custom-call | tf_op jit(solution)/shard_map/conv_attention_backward/pallas_call | solution.py:727
  64.3 1.7 %store_results.1 = (bf16[128,256]{1,0:T(8,128)(2,1)}, bf16[128,256]{1,0:T(8,128)(2,1)}, bf16[128,256]{1,0:T(8,128)(2,1)}, bf16[128,256]{1,0:T(8,128)(2,1)}, f32[16,256]{1,0:T(8,128)}, /*index=5*/f32[31,256]{1,0:T(8,128)}) custom-call(bf16[128,256]{1,0:T(8,128)(2,1)} %get-tuple-element.12.refs_0_, bf16[128,256]{1,0:T(8,128)(2,1)} %get-tuple-element.13.refs_1_, ...), custom_call_target="tpu_custom_call" | custom-call | tf_op jit(solution)/shard_map/store_results/pallas_call | solution.py:738
